TPU v7x, 32 devices: a whole 2x2x4 slice. The times are simulated.
32 devices in a mesh: dp: 8 (over y, x, core), branch: 4 (over z).
Axes of the slice: x: 2, y: 2, z: 4, core: 2. Of those that a mesh axis runs over, the one named last changes fastest.
Arguments:
- block_input: bfloat16 [8, 1024, 2048], P('dp', 'branch'), may hold values from -6 to 6
- segment_ids: int32 [8, 1024], P('dp'), may hold values from 0 to 3, as said below
- out_cotangent: bfloat16 [8, 1024, 2048], P('dp', 'branch'), may hold values from -6 to 6
- norm_gain: float32 [2048], replicated, may hold values from 0.5 to 1.5
- norm_bias: float32 [2048], replicated, may hold values from -1.75 to 1.75
- query_weight: bfloat16 [2048, 2048], P('dp', 'branch'), may hold values from -0.125 to 0.125
- key_weight: bfloat16 [2048, 2048], P('dp', 'branch'), may hold values from -0.125 to 0.125
- value_weight: bfloat16 [2048, 2048], P('dp', 'branch'), may hold values from -0.125 to 0.125
- query_bias: float32 [2048], P('branch'), may hold values from -1.75 to 1.75
- key_bias: float32 [2048], P('branch'), may hold values from -1.75 to 1.75
- value_bias: float32 [2048], P('branch'), may hold values from -1.75 to 1.75
- out_weight: bfloat16 [2048, 2048], P('branch', 'dp'), may hold values from -1.5 to 1.5
- fc1_weight: bfloat16 [2048, 8192], P('dp', 'branch'), may hold values from -0.125 to 0.125
- fc1_bias: float32 [8192], P('branch'), may hold values from -3 to 3
- fc2_weight: bfloat16 [8192, 2048], P('branch', 'dp'), may hold values from -0.0625 to 0.0625
- output_bias: float32 [2048], replicated, may hold values from -3 to 3
Outputs:
- block_output: bfloat16 [8, 1024, 2048], P('dp', 'branch')
- input_grad: float32 [8, 1024, 2048], P('dp', 'branch')
- gain_grad: float32 [2048], replicated
- norm_bias_grad: float32 [2048], replicated
- query_weight_grad: float32 [2048, 2048], P('dp', 'branch')
- key_weight_grad: float32 [2048, 2048], P('dp', 'branch')
- value_weight_grad: float32 [2048, 2048], P('dp', 'branch')
- query_bias_grad: float32 [2048], P('branch')
- key_bias_grad: float32 [2048], P('branch')
- value_bias_grad: float32 [2048], P('branch')
- out_weight_grad: float32 [2048, 2048], P('branch', 'dp')
- fc1_weight_grad: float32 [2048, 8192], P('dp', 'branch')
- fc1_bias_grad: float32 [8192], P('branch')
- fc2_weight_grad: float32 [8192, 2048], P('branch', 'dp')
- output_bias_grad: float32 [2048], replicated
Inputs may be any that keep to these rules, and one draw needn't show every extreme that they name: `segment_ids`: in each row of 1024 tokens the values are 1, 2, 3, 0 in runs of that order: documents 1 and 2 (1 may be empty) lie within the first 128 tokens, document 3 begins there and ends within the last 64 tokens, and padding 0 fills the rest, one token or more.
All inputs are finite; a program needn't handle non-finite values.
Results may differ from a plain program's by a relative error of at most 0.012.
The roundings to bfloat16 on the way count: a program that leaves them out, or rounds other values in their place, can miss the bound.
Values may be sent and summed in bfloat16 or wider, within the bound.
A program may use at most 256 MiB of HBM per device.

v0:
```python
import functools

import jax
import jax.numpy as jnp
from jax import lax
from jax.experimental import pallas as pl
from jax.experimental.pallas import tpu as pltpu
from jax.sharding import PartitionSpec as P

HEAD_DIM = 64
ROT = 32
EPSILON = 1e-05
NEGATIVE = -1e30
LANES = 128
TILE = 512
QBLOCK = 256
MESH = pl.DeviceIdType.MESH
BF16 = jnp.bfloat16
F32 = jnp.float32
GELU_C = 0.7978845608028654
GELU_A = 0.044715
VMEM_LIMIT = 60 * 1024 * 1024 + 512 * 1024


def flip(index, bits):
    out = index
    bit = 1
    while bit <= bits:
        if bits & bit:
            out = out + bit * (1 - 2 * lax.rem(lax.div(index, bit), 2))
        bit *= 2
    return out


def dot_nn(left, right):
    return jnp.dot(left, right, preferred_element_type=F32)


def dot_nt(left, right):
    return lax.dot_general(left, right, (((1,), (1,)), ((), ())), preferred_element_type=F32)


def tile_of(extent, most=TILE):
    return min(most, extent)


def aligned(index, step):
    return pl.ds(pl.multiple_of(index * step, step), step)


class Chain:
    def __init__(self, own_src, buf, rows, count, sems, dp):
        self.own_src, self.buf, self.rows, self.count = own_src, buf, rows, count
        self.sems, self.dp = sems, dp
        self.z = lax.axis_index("branch")

    def block(self, slot):
        return self.buf.at[aligned(slot, self.rows), :]

    def copy(self, up, step, slot, src=None):
        send, recv = self.sems[0 if up else 2], self.sems[1 if up else 3]
        return pltpu.make_async_remote_copy(
            src_ref=self.block(slot) if src is None else src,
            dst_ref=self.block(slot),
            send_sem=send.at[step],
            recv_sem=recv.at[step],
            device_id=(self.dp, self.z + 1 if up else self.z - 1),
            device_id_type=MESH,
        )

    def sends(self, up, step):
        z, last = self.z, self.count - 1
        if up:
            return jnp.logical_and(z >= step, z < last)
        return jnp.logical_and(z + step <= last, z > 0)

    def sent_slot(self, up, step):
        return self.z - step if up else self.z + step

    def start(self):
        for up in (False, True):

            @pl.when(self.sends(up, 0))
            def _(up=up):
                self.copy(up, 0, self.z, self.own_src).start()

    def pump(self, step):
        for up in (False, True):

            @pl.when(self.sends(up, step))
            def _(up=up):
                slot = self.sent_slot(up, step)
                self.copy(up, step - 1, slot).wait_recv()
                self.copy(up, step, slot).start()

    def by_distance(self, first, end, work):
        def visit(i, _):
            far = lax.div(i + 1, 2)
            above = lax.rem(i, 2) == 0
            slot = self.z + jnp.where(above, far, -far)

            @pl.when(jnp.logical_and(slot >= 0, slot <= self.count - 1))
            def _():
                for up in (False, True):
                    mine = jnp.logical_and(far > 0, above if not up else jnp.logical_not(above))

                    @pl.when(jnp.logical_and(mine, jnp.logical_not(self.sends(up, far))))
                    def _(up=up):
                        self.copy(up, far - 1, slot).wait_recv()

                work(slot)

            return 0

        lax.fori_loop(first, end, visit, 0)

    def finish(self):
        for step in range(self.count - 1):
            for up in (False, True):

                @pl.when(self.sends(up, step))
                def _(up=up, step=step):
                    self.copy(up, step, self.sent_slot(up, step), self.own_src if step == 0 else None).wait_send()


class Gather:
    def __init__(self, index, shard, full, by_rows, chips, sems):
        self.index, self.shard, self.full = index, shard, full
        self.by_rows, self.chips = by_rows, chips
        self.send, self.recv, self.relay_send, self.relay_recv, self.pair_send, self.pair_recv, self.own = sems
        dp = lax.axis_index("dp")
        self.z = lax.axis_index("branch")
        self.core = lax.rem(dp, 2)
        self.chip = lax.div(dp, 2)
        self.width = shard.shape[0 if by_rows else 1]
        self.relayed = chips == 4
        self.direct = (1, 2) if self.relayed else tuple(range(1, chips))

    def slot(self, dp):
        part = aligned(dp, self.width)
        return self.full.at[part, :] if self.by_rows else self.full.at[:, part]

    def half(self, dp, which):
        if self.by_rows:
            return self.full.at[aligned(2 * dp + which, self.width // 2), :]
        rows = self.shard.shape[0] // 2
        return self.full.at[pl.ds(which * rows, rows), aligned(dp, self.width)]

    def at(self, r, core):
        return flip(self.chip, r) * 2 + core

    def to_chip(self, r, landing):
        return pltpu.make_async_remote_copy(
            src_ref=self.shard,
            dst_ref=self.slot(landing),
            send_sem=self.send.at[self.index, r - 1],
            recv_sem=self.recv.at[self.index, r - 1],
            device_id=(self.at(r, self.core), self.z),
            device_id_type=MESH,
        )

    def relay(self, which, owner):
        return pltpu.make_async_remote_copy(
            src_ref=self.half(owner, which),
            dst_ref=self.half(owner, which),
            send_sem=self.relay_send.at[self.index, which],
            recv_sem=self.relay_recv.at[self.index, which],
            device_id=(self.at(2 - which, self.core), self.z),
            device_id_type=MESH,
        )

    def to_pair(self, r, landing):
        return pltpu.make_async_remote_copy(
            src_ref=self.shard if r == 0 else self.slot(self.at(r, self.core)),
            dst_ref=self.slot(landing),
            send_sem=self.pair_send.at[self.index, r],
            recv_sem=self.pair_recv.at[self.index, r],
            device_id=(self.chip * 2 + 1 - self.core, self.z),
            device_id_type=MESH,
        )

    def fetch(self):
        return pltpu.make_async_copy(self.shard, self.slot(self.at(0, self.core)), self.own.at[self.index])

    def start(self):
        for r in self.direct:
            self.to_chip(r, self.at(0, self.core)).start()

    def start_pair(self):
        self.to_pair(0, self.at(0, self.core)).start()
        self.fetch().start()

    def land(self):
        for r in self.direct:
            owner = self.at(r, self.core)
            self.to_chip(r, owner).wait_recv()
            if self.relayed:
                self.relay(r - 1, owner).start()
            self.to_pair(r, owner).start()

    def land_last(self):
        if self.relayed:
            owner = self.at(3, self.core)
            for which in range(2):
                self.relay(which, owner).wait_recv()
            self.to_pair(3, owner).start()

    def arrive(self):
        self.fetch().wait()
        for r in range(self.chips):
            self.to_pair(r, self.at(r, 1 - self.core)).wait_recv()

    def finish(self):
        for r in self.direct:
            self.to_chip(r, self.at(0, self.core)).wait_send()
            if self.relayed:
                self.relay(r - 1, self.at(r, self.core)).wait_send()
        for r in range(self.chips):
            self.to_pair(r, self.at(r, self.core)).wait_send()


def greet(chips, count):
    dp, z = lax.axis_index("dp"), lax.axis_index("branch")
    core, chip = lax.rem(dp, 2), lax.div(dp, 2)
    barrier = pltpu.get_barrier_semaphore()
    for r in range(1, chips):
        pl.semaphore_signal(barrier, inc=1, device_id=(flip(chip, r) * 2 + core, z), device_id_type=MESH)
    pl.semaphore_signal(barrier, inc=1, device_id=(chip * 2 + 1 - core, z), device_id_type=MESH)
    for shift in range(1, count):
        pl.semaphore_signal(barrier, inc=1, device_id=(dp, lax.rem(z + shift, count)), device_id_type=MESH)
    pl.semaphore_wait(barrier, chips + count - 1)


def swapped(y):
    lane = lax.rem(lax.broadcasted_iota(jnp.int32, y.shape, 1), HEAD_DIM)
    return jnp.where(lane < ROT // 2, pltpu.roll(y, LANES - ROT // 2, 1), pltpu.roll(y, ROT // 2, 1))


def forward_kernel(
    chips, count,
    x, gain, beta, bqkv, bf1, seg_row, frequency, wq, wk, wv, wf1, wo, wf2, cot,
    gqkv, gf1, gcot, hid_t, qkv_out, att_t_out, lse_out, act_t, pre_out, part_out, att_grad_out, table_c, table_s, seg_col, sums,
    hid, vqkv, vf1, vf2, vo, qkv, att, att_t, lse, act, dg, part, stage, g_rows, att_grad, tab_c, tab_s, segs,
    w_send, w_recv, r_send, r_recv, p_send, p_recv, own_sem,
    h_us, h_ur, h_ds, h_dr, c_us, c_ur, c_ds, c_dr, cot_sem, save_sem, st_sem,
):
    z = lax.axis_index("branch")
    dp = lax.axis_index("dp")
    rows, width = x.shape
    length = rows * count
    hcols = wo.shape[0]
    units = wf2.shape[0]
    sems = (w_send, w_recv, r_send, r_recv, p_send, p_recv, own_sem)
    g_qkv = [
        Gather(n, w, vqkv.at[:, n * hcols : (n + 1) * hcols], True, chips, sems) for n, w in enumerate((wq, wk, wv))
    ]
    g_f1 = Gather(3, wf1, vf1, True, chips, sems)
    g_o = Gather(4, wo, vo, False, chips, sems)
    g_f2 = Gather(5, wf2, vf2, False, chips, sems)
    h_chain = Chain(hid.at[aligned(z, rows), :], hid, rows, count, (h_us, h_ur, h_ds, h_dr), dp)
    c_chain = Chain(cot, gcot, rows, count, (c_us, c_ur, c_ds, c_dr), dp)
    saves = []

    def save(src, dst):
        c = pltpu.make_async_copy(src, dst, save_sem.at[len(saves)])
        c.start()
        saves.append(c)

    greet(chips, count)
    for g in (*g_qkv, g_f1):
        g.start()
    for g in (*g_qkv, g_f1, g_o, g_f2):
        g.start_pair()
    own_cot = g_rows.at[0:rows, :]
    fetch_cot = pltpu.make_async_copy(cot, own_cot, cot_sem.at[0])
    fetch_cot.start()

    step_rows = 32

    def norm(i, _):
        part_rows = aligned(i, step_rows)
        inputs = x[part_rows, :].astype(F32)
        center = inputs - jnp.mean(inputs, axis=-1, keepdims=True)
        inverse = lax.rsqrt(jnp.mean(center * center, axis=-1, keepdims=True) + EPSILON)
        where = pl.ds(pl.multiple_of(z * rows + i * step_rows, step_rows), step_rows)
        hid[where, :] = (center * inverse * gain[...] + beta[...]).astype(BF16)
        return 0

    lax.fori_loop(0, rows // step_rows, norm, 0)
    h_chain.start()
    fetch_cot.wait()
    save(own_cot, gcot.at[aligned(z, rows), :])

    row_segs = seg_row[...].astype(F32)
    places = lax.broadcasted_iota(jnp.int32, (1, length), 1).astype(F32)
    firsts = [
        jnp.min(jnp.where(row_segs == float(value), places, float(length)), axis=1, keepdims=True)
        for value in range(4)
    ]
    for c in range(length // LANES):
        here = slice(c * LANES, (c + 1) * LANES)
        seg = jnp.broadcast_to(row_segs[:, here], (LANES, LANES)).T
        segs[here, :] = seg
        start = jnp.zeros((LANES, LANES), F32)
        for value in range(4):
            start = jnp.where(seg == float(value), firsts[value], start)
        place = (lax.broadcasted_iota(jnp.int32, (LANES, LANES), 0) + c * LANES).astype(F32)
        angle = (place - start) * frequency[...]
        lane = lax.rem(lax.broadcasted_iota(jnp.int32, (LANES, LANES), 1), HEAD_DIM)
        sine = jnp.where(lane < ROT, jnp.sin(angle), 0.0)
        tab_c[here, :] = jnp.where(lane < ROT, jnp.cos(angle), 1.0)
        tab_s[here, :] = jnp.where(lane < ROT // 2, -sine, sine)
    key_row = jnp.where(row_segs == 0.0, -1.0, row_segs)
    save(tab_c, table_c)
    save(tab_s, table_s)
    save(segs, seg_col)

    for g in g_qkv:
        g.land()
    for g in (g_o, g_f2):
        g.start()
    if count > 2:
        h_chain.pump(1)
    g_f1.land()
    for s in range(2, count - 1):
        h_chain.pump(s)
    c_chain.start()
    for g in g_qkv:
        g.land_last()
    for g in g_qkv:
        g.arrive()
    save(vqkv, gqkv)

    ht, wt = tile_of(hcols), tile_of(width)

    def turn_copy(slot, j, cols_i):
        return pltpu.make_async_copy(
            stage.at[slot, pl.ds(0, wt), pl.ds(0, rows)], hid_t.at[cols_i, aligned(j, rows)], st_sem.at[slot]
        )

    def project(j):
        rows_j = aligned(j, rows)
        for which in range(3):
            for c in range(hcols // ht):
                at = which * hcols + c * ht
                y = dot_nn(hid[rows_j, :], vqkv[:, at : at + ht]) + bqkv[:, at : at + ht]
                for piece in range(ht // LANES):
                    part_y = y[:, piece * LANES : (piece + 1) * LANES]
                    if which < 2:
                        part_y = part_y * tab_c[rows_j, :] + swapped(part_y) * tab_s[rows_j, :]
                    low = part_y.astype(BF16)
                    if which == 0:
                        low = low * BF16(HEAD_DIM**-0.5)
                    qkv[rows_j, at + piece * LANES : at + (piece + 1) * LANES] = low

        def turn(i, _):
            cols_i, slot = aligned(i, wt), lax.rem(i, 2)

            @pl.when(i >= 2)
            def _():
                turn_copy(slot, j, cols_i).wait()

            stage[slot, 0:wt, 0:rows] = hid[rows_j, cols_i].T
            turn_copy(slot, j, cols_i).start()
            return 0

        n_turn = width // wt
        lax.fori_loop(0, n_turn, turn, 0)
        for i in range(max(n_turn - 2, 0), n_turn):
            turn_copy(i % 2, j, pl.ds(0, wt)).wait()

    h_chain.by_distance(0, 2 * count - 3, project)
    g_o.land()
    h_chain.by_distance(2 * count - 3, 2 * count - 1, project)
    save(qkv, qkv_out)
    g_f2.land()
    if count > 2:
        c_chain.pump(1)

    qb = tile_of(length, QBLOCK)
    pairs = hcols // LANES

    def attend(pair, _):
        cols = aligned(pair, LANES)
        k_cols, v_cols = aligned(pairs + pair, LANES), aligned(2 * pairs + pair, LANES)
        lane = lax.broadcasted_iota(jnp.int32, (1, LANES), 1)
        for b in range(length // qb):
            here = slice(b * qb, (b + 1) * qb)
            before = b * qb
            q2 = qkv[here, cols]
            seg_q = segs[here, 0:1]
            ki = lax.broadcasted_iota(jnp.int32, (qb, qb), 1)
            qi = lax.broadcasted_iota(jnp.int32, (qb, qb), 0)
            seen_here = jnp.logical_or(jnp.logical_and(seg_q == key_row[:, here], ki <= qi), ki == qi)
            out = jnp.zeros((qb, LANES), F32)
            stat = jnp.zeros((qb, LANES), F32)
            for h in range(2):
                mine = (lane // HEAD_DIM) == h
                qh = jnp.where(mine, q2, BF16(0))
                s_here = jnp.where(seen_here, dot_nt(qh, qkv[here, k_cols]), NEGATIVE)
                top = jnp.max(s_here, axis=-1, keepdims=True)
                if before:
                    s_before = jnp.where(
                        seg_q == key_row[:, :before], dot_nt(qh, qkv[:before, k_cols]), NEGATIVE
                    )
                    top = jnp.maximum(top, jnp.max(s_before, axis=-1, keepdims=True))
                e_here = jnp.exp(s_here - top)
                total = jnp.sum(e_here, axis=-1, keepdims=True)
                if before:
                    e_before = jnp.exp(s_before - top)
                    total = total + jnp.sum(e_before, axis=-1, keepdims=True)
                share = 1.0 / total
                o = dot_nn((e_here * share).astype(BF16), jnp.where(mine, qkv[here, v_cols], BF16(0)))
                if before:
                    o = o + dot_nn(
                        (e_before * share).astype(BF16), jnp.where(mine, qkv[:before, v_cols], BF16(0))
                    )
                out = out + o
                stat = jnp.where(mine, top + jnp.log(total), stat)
            att[here, cols] = out.astype(BF16)
            att_t[cols, here] = out.T.astype(BF16)
            turned = stat.T
            lse[pl.ds(2 * pair, 1), here] = turned[0:1, :]
            lse[pl.ds(2 * pair + 1, 1), here] = turned[HEAD_DIM : HEAD_DIM + 1, :]
        return 0

    half_pairs = pairs // 2
    lax.fori_loop(0, half_pairs, attend, 0)
    for s in range(2, count - 1):
        c_chain.pump(s)
    lax.fori_loop(half_pairs, pairs - 1, attend, 0)
    g_f1.land_last()
    lax.fori_loop(pairs - 1, pairs, attend, 0)
    save(att_t, att_t_out)
    save(lse, lse_out)
    g_f1.arrive()
    save(vf1, gf1)

    mt, ft = tile_of(length), tile_of(units)
    per_row = units // ft
    n_tiles = (length // mt) * per_row

    def staged(slot, rows_i, cols_i):
        return pltpu.make_async_copy(stage.at[slot, pl.ds(0, ft), :], act_t.at[cols_i, rows_i], st_sem.at[slot])

    def unit(i, _):
        rows_i, cols_i = aligned(lax.div(i, per_row), mt), aligned(lax.rem(i, per_row), ft)
        slot = lax.rem(i, 2)

        @pl.when(i >= 2)
        def _():
            staged(slot, rows_i, cols_i).wait()

        y = dot_nn(hid[rows_i, :], vf1[:, cols_i]) + bf1[:, cols_i]
        square = y * y
        t = jnp.tanh(GELU_C * (y + GELU_A * (y * square)))
        half = 0.5 * (1.0 + t)
        low = (y * half).astype(BF16)
        act[rows_i, cols_i] = low
        stage[slot, 0:ft, :] = low.T
        dg[rows_i, cols_i] = (
            half + 0.5 * y * (1.0 - t * t) * (GELU_C * (1.0 + 3.0 * GELU_A * square))
        ).astype(BF16)
        staged(slot, rows_i, cols_i).start()
        return 0

    half_tiles = n_tiles // 2
    lax.fori_loop(0, half_tiles, unit, 0)
    for g in (g_o, g_f2):
        g.land_last()
    lax.fori_loop(half_tiles, n_tiles, unit, 0)
    for i in range(max(n_tiles - 2, 0), n_tiles):
        staged(i % 2, pl.ds(0, mt), pl.ds(0, ft)).wait()
    for g in (g_o, g_f2):
        g.arrive()

    def output(i, _):
        rows_i, cols_i = aligned(lax.div(i, width // wt), mt), aligned(lax.rem(i, width // wt), wt)
        part[rows_i, cols_i] = (
            dot_nn(act[rows_i, :], vf2[:, cols_i]) + dot_nn(att[rows_i, :], vo[:, cols_i])
        ).astype(BF16)
        return 0

    lax.fori_loop(0, (length // mt) * (width // wt), output, 0)
    save(part, part_out)
    saves[0].wait()

    sums[...] = jnp.zeros_like(sums)

    def unit_back(j):
        rows_j = aligned(j, rows)
        fetch = pltpu.make_async_copy(gcot.at[rows_j, :], g_rows, cot_sem.at[0])
        fetch.start()
        fetch.wait()

        def body(i, _):
            cols_i = aligned(i, ft)
            low = (dot_nt(g_rows[...], vf2[cols_i, :]) * dg[rows_j, cols_i].astype(F32)).astype(BF16)
            dg[rows_j, cols_i] = low
            sums[:, cols_i] += jnp.sum(low.astype(F32), axis=0, keepdims=True)
            return 0

        lax.fori_loop(0, per_row, body, 0)
        att_grad[rows_j, :] = dot_nt(g_rows[...], vo[...]).astype(BF16)
        sums[:, units : units + width] += jnp.sum(g_rows[...].astype(F32), axis=0, keepdims=True)

    c_chain.by_distance(0, 2 * count - 1, unit_back)
    save(dg, pre_out)
    save(att_grad, att_grad_out)
    for g in (*g_qkv, g_f1, g_o, g_f2):
        g.finish()
    h_chain.finish()
    c_chain.finish()
    for c in saves[1:]:
        c.wait()


def run_forward(ndp, count, x, gain, beta, bqkv, bf1, seg_row, frequency, wq, wk, wv, wf1, wo, wf2, cot):
    chips = ndp // 2
    rows, width = x.shape
    length = rows * count
    hcols, units = wo.shape[0], wf2.shape[0]
    heads = hcols // HEAD_DIM
    mt, ft, wt = tile_of(length), tile_of(units), tile_of(width)
    anywhere = pl.BlockSpec(memory_space=pl.ANY)
    vmem = pl.BlockSpec(memory_space=pltpu.VMEM)
    low = lambda *shape: jax.ShapeDtypeStruct(shape, BF16)
    wide = lambda *shape: jax.ShapeDtypeStruct(shape, F32)
    outs = [
        low(width, 3 * hcols), low(width, units), low(length, width), low(width, length), low(length, 3 * hcols),
        low(hcols, length), wide(heads, length), low(units, length), low(length, units), low(length, width), low(length, hcols),
        wide(length, LANES), wide(length, LANES), wide(length, LANES), wide(1, units + width),
    ]
    v = lambda *shape: pltpu.VMEM(shape, BF16)
    w = lambda *shape: pltpu.VMEM(shape, F32)
    steps = max(count - 1, 1)
    dma = lambda *shape: pltpu.SemaphoreType.DMA(shape)
    scratch = [
        v(length, width), v(width, 3 * hcols), v(width, units), v(units, width), v(hcols, width),
        v(length, 3 * hcols), v(length, hcols), v(hcols, length), w(heads, length), v(length, units), v(length, units),
        v(length, width), v(2, max(ft, wt), mt), v(rows, width), v(length, hcols),
        w(length, LANES), w(length, LANES), w(length, LANES),
        dma(6, chips - 1), dma(6, chips - 1), dma(6, 2), dma(6, 2), dma(6, chips), dma(6, chips), dma(6),
        *[dma(steps) for _ in range(8)], dma(1), dma(16), dma(2),
    ]
    return pl.pallas_call(
        functools.partial(forward_kernel, chips, count),
        out_shape=outs,
        in_specs=[vmem] * 7 + [anywhere] * 7,
        out_specs=[anywhere] * (len(outs) - 1) + [vmem],
        scratch_shapes=scratch,
        compiler_params=pltpu.CompilerParams(
            collective_id=0, has_side_effects=True, vmem_limit_bytes=VMEM_LIMIT
        ),
        name="gather_forward",
    )(x, gain, beta, bqkv, bf1, seg_row, frequency, wq, wk, wv, wf1, wo, wf2, cot)


class Fold:
    def __init__(self, bufs, sems, count, dp):
        self.bufs, self.sems, self.count, self.dp = bufs, sems, count, dp
        self.z = lax.axis_index("branch")

    def place(self, up):
        return self.z if up else self.count - 1 - self.z

    def dest(self, up, step):
        return self.count - 1 - step if up else step

    def hop(self, up, step, src=None):
        buf = self.bufs[0 if up else 1]
        send, recv = self.sems[0 if up else 2], self.sems[1 if up else 3]
        return pltpu.make_async_remote_copy(
            src_ref=buf.at[step] if src is None else src,
            dst_ref=buf.at[step],
            send_sem=send.at[step],
            recv_sem=recv.at[step],
            device_id=(self.dp, self.z + 1 if up else self.z - 1),
            device_id_type=MESH,
        )

    def first(self, up, step, src):
        @pl.when(self.place(up) == 0)
        def _():
            self.hop(up, step, src).start()

    def pump(self, k, own_block, rows):
        for up in (False, True):
            place = self.place(up)

            @pl.when(jnp.logical_and(place >= 1, place <= k))
            def _(up=up, place=place):
                step = k - place
                own = own_block(up, self.dest(up, step))
                self.hop(up, step).wait_recv()
                buf = self.bufs[0 if up else 1]

                def add(i, _):
                    part = aligned(i, 32)
                    buf[step, part, :] = (buf[step, part, :].astype(F32) + own[part, :].astype(F32)).astype(BF16)
                    return 0

                lax.fori_loop(0, rows // 32, add, 0)
                self.hop(up, step).start()

    def last_step(self, up):
        return jnp.clip(self.count - 1 - self.place(up), 0, self.count - 2)

    def arrive(self):
        for up in (False, True):

            @pl.when(self.place(up) >= 1)
            def _(up=up):
                self.hop(up, self.last_step(up)).wait_recv()

    def total(self, own, part):
        out = own
        for up in (False, True):
            got = self.bufs[0 if up else 1][self.last_step(up), part, :].astype(F32)
            out = out + jnp.where(self.place(up) >= 1, got, 0.0)
        return out

    def finish(self):
        for step in range(self.count - 1):
            for up in (False, True):

                @pl.when(self.place(up) + step <= self.count - 2)
                def _(up=up, step=step):
                    self.hop(up, step).wait_send()


class Scatter:
    def __init__(self, index, block, tile, rows_first, slots, landing, own_out, stage, wide, chips, sems):
        self.index, self.block, self.tile, self.rows_first = index, block, tile, rows_first
        self.slots, self.landing, self.own_out, self.stage, self.wide = slots, landing, own_out, stage, wide
        self.chips = chips
        self.st_sem, self.pair_recv, self.send, self.recv, self.wide_sem = sems
        dp = lax.axis_index("dp")
        self.z = lax.axis_index("branch")
        self.core, self.chip = lax.rem(dp, 2), lax.div(dp, 2)
        self.tiles = slots.shape[2 if rows_first else 1] // tile
        self.height = slots.shape[1] if rows_first else tile
        self.breadth = tile if rows_first else slots.shape[2]
        self.order = [*range(1, chips), 0]

    def part(self, ref, i):
        at = aligned(i, self.tile)
        return ref.at[:, at] if self.rows_first else ref.at[at, :]

    def view(self, ref, slot):
        return ref.at[slot, pl.ds(0, self.height), pl.ds(0, self.breadth)]

    def to_pair(self, r, i, slot):
        return pltpu.make_async_remote_copy(
            src_ref=self.view(self.stage, slot),
            dst_ref=self.part(self.slots.at[r], i),
            send_sem=self.st_sem.at[slot],
            recv_sem=self.pair_recv.at[self.index, r],
            device_id=(self.chip * 2 + 1 - self.core, self.z),
            device_id_type=MESH,
        )

    def from_pair(self, r):
        return pltpu.make_async_remote_copy(
            src_ref=self.slots.at[r],
            dst_ref=self.slots.at[r],
            send_sem=self.st_sem.at[0],
            recv_sem=self.pair_recv.at[self.index, r],
            device_id=(self.chip * 2 + 1 - self.core, self.z),
            device_id_type=MESH,
        )

    def to_owner(self, r):
        return pltpu.make_async_remote_copy(
            src_ref=self.slots.at[r],
            dst_ref=self.landing.at[r - 1],
            send_sem=self.send.at[self.index, r - 1],
            recv_sem=self.recv.at[self.index, r - 1],
            device_id=(flip(self.chip, r) * 2 + self.core, self.z),
            device_id_type=MESH,
        )

    def to_out(self, i, slot):
        return pltpu.make_async_copy(self.view(self.wide, slot), self.part(self.own_out, i), self.wide_sem.at[slot])

    def partners(self, n):
        r = self.order[n]
        owner = flip(self.chip, r) * 2 + 1 - self.core

        def body(i, _):
            slot = lax.rem(n * self.tiles + i, 2)
            y = self.block(owner, i)
            if n * self.tiles >= 2:
                self.to_pair(r, i, slot).wait_send()
            else:

                @pl.when(n * self.tiles + i >= 2)
                def _():
                    self.to_pair(r, i, slot).wait_send()

            self.stage[slot, 0 : self.height, 0 : self.breadth] = y.astype(BF16)
            self.to_pair(r, i, slot).start()
            return 0

        lax.fori_loop(0, self.tiles, body, 0)

    def own(self, n):
        r = self.order[n]
        owner = flip(self.chip, r) * 2 + self.core
        self.from_pair(r).wait_recv()

        def body(i, _):
            y = self.block(owner, i)
            at = aligned(i, self.tile)
            if self.rows_first:
                y = y + self.slots[r, :, at].astype(F32)
            else:
                y = y + self.slots[r, at, :].astype(F32)
            if r:
                if self.rows_first:
                    self.slots[r, :, at] = y.astype(BF16)
                else:
                    self.slots[r, at, :] = y.astype(BF16)
            else:
                slot = lax.rem(i, 2)

                @pl.when(i >= 2)
                def _():
                    self.to_out(i, slot).wait()

                self.wide[slot, 0 : self.height, 0 : self.breadth] = y
                self.to_out(i, slot).start()
            return 0

        lax.fori_loop(0, self.tiles, body, 0)
        if r:
            self.to_owner(r).start()
        else:
            for i in range(max(self.tiles - 2, 0), self.tiles):
                self.to_out(i, i % 2).wait()

    def run(self, before=lambda n: None):
        for n in range(self.chips):
            before(n)
            self.partners(n)
            if n:
                self.own(n - 1)
        self.own(self.chips - 1)
        total = self.chips * self.tiles
        for i in range(max(total - 2, 0), total):
            self.to_pair(0, 0, i % 2).wait_send()

    def finish(self):
        for r in range(1, self.chips):
            self.to_owner(r).wait_send()
            self.to_owner(r).wait_recv()


def piece_of(extent):
    return next(n for n in (512, 256, 128) if extent % n == 0)


def backward_kernel(
    chips, count,
    gqkv, gf1, gcot, hid_t, qkv_in, att_t, act_t, pre_in, part_in, att_grad_in, x_in,
    lse, gain, out_bias, table_c, table_s, seg_row, seg_col, sums,
    block_out, input_grad, vec_out, own_qkv, own_f1, own_o, own_f2, land_qkv, land_f1, land_o, land_f2,
    g, pre, f1_v, mid, qkv, att_grad, dk_acc, dv_acc, k_t, hid_stage, tmp, s_qkv, s_f1, s_o, s_f2, up_buf, dn_buf,
    st_row, st_col, wide_row, wide_col, ig_stage, vec, vec_pair, vec_chip, vec_z,
    load_sem, hid_sem, tmp_sem, out_sem, ig_sem, st_row_sem, st_col_sem, pair_recv, x_send, x_recv, wide_row_sem, wide_col_sem,
    zo_us, zo_ur, zo_ds, zo_dr, zh_us, zh_ur, zh_ds, zh_dr, free_up, free_dn, v_ps, v_pr, v_cs, v_cr, v_zs, v_zr,
):
    z = lax.axis_index("branch")
    dp = lax.axis_index("dp")
    core, chip = lax.rem(dp, 2), lax.div(dp, 2)
    length, width = g.shape
    rows = length // count
    hcols, units = att_t.shape[0], act_t.shape[0]
    part_w = width // (2 * chips)
    last = count - 1
    wt = tile_of(width)
    act_v, att_v, wqkv_v = mid.at[0:units, 0:length], mid.at[0:hcols, 0:length], mid.at[0:width, 0 : 3 * hcols]

    def load(src, dst, n):
        c = pltpu.make_async_copy(src, dst, load_sem.at[n])
        c.start()
        return c

    load_g = load(gcot, g, 0)
    load_act = load(act_t, act_v, 1)
    load_qkv = load(qkv_in, qkv, 2)
    load_att_grad = load(att_grad_in, att_grad, 3)
    load_pre = load(pre_in, pre, 4)
    load_f1 = load(gf1, f1_v, 5)
    greet(chips, count)

    def rows_of(ref, d):
        return ref.at[aligned(d, rows), :]

    fold_out = Fold((up_buf, dn_buf), (zo_us, zo_ur, zo_ds, zo_dr), count, dp)
    fold_hid = Fold((up_buf, dn_buf), (zh_us, zh_ur, zh_ds, zh_dr), count, dp)
    for s in range(count - 1):
        fold_out.first(True, s, rows_of(part_in, last - s))
        fold_out.first(False, s, rows_of(part_in, s))

    def fetched(up, d):
        n = 0 if up else 1
        c = pltpu.make_async_copy(rows_of(part_in, d), tmp.at[n], tmp_sem.at[n])
        c.start()
        c.wait()
        return tmp.at[n]

    sems_row = (st_row_sem, pair_recv, x_send, x_recv, wide_row_sem)
    sems_col = (st_col_sem, pair_recv, x_send, x_recv, wide_col_sem)
    tile_f2, tile_o = piece_of(units), piece_of(hcols)
    tile_f1, tile_qkv = piece_of(units), piece_of(3 * hcols)

    def f2_block(owner, i):
        return dot_nn(act_v[aligned(i, tile_f2), :], g[:, aligned(owner, part_w)])

    def o_block(owner, i):
        return dot_nn(att_v[aligned(i, tile_o), :], g[:, aligned(owner, part_w)])

    def hid_copy(n, which, r, slot_core):
        owner = flip(chip, r) * 2 + slot_core
        return pltpu.make_async_copy(
            hid_t.at[aligned(owner, part_w), :], hid_stage.at[2 * which + n % 2], hid_sem.at[2 * which + n % 2]
        )

    state = {}

    def f1_block(owner, i):
        return dot_nn(hid_stage[state["at"]], pre[:, aligned(i, tile_f1)])

    def qkv_block(owner, i):
        return dot_nn(hid_stage[state["at"]], qkv[:, aligned(i, tile_qkv)])

    def run_rows(scatter):
        order = scatter.order
        hid_copy(0, 0, order[0], 1 - core).start()
        hid_copy(0, 1, order[0], core).start()
        for n in range(chips):
            if n + 1 < chips:
                hid_copy(n + 1, 0, order[n + 1], 1 - core).start()
            hid_copy(n, 0, order[n], 1 - core).wait()
            state["at"] = n % 2
            scatter.partners(n)
            if n:
                hid_copy(n, 1, order[n], core).start()
                hid_copy(n - 1, 1, order[n - 1], core).wait()
                state["at"] = 2 + (n - 1) % 2
                scatter.own(n - 1)
        hid_copy(chips - 1, 1, order[chips - 1], core).wait()
        state["at"] = 2 + (chips - 1) % 2
        scatter.own(chips - 1)
        total = chips * scatter.tiles
        for i in range(max(total - 2, 0), total):
            scatter.to_pair(0, 0, i % 2).wait_send()

    sc_f2 = Scatter(0, f2_block, tile_f2, False, s_f2, land_f2, own_f2, st_col, wide_col, chips, sems_col)
    sc_f1 = Scatter(1, f1_block, tile_f1, True, s_f1, land_f1, own_f1, st_row, wide_row, chips, sems_row)
    sc_o = Scatter(2, o_block, tile_o, False, s_o, land_o, own_o, st_col, wide_col, chips, sems_col)
    sc_qkv = Scatter(3, qkv_block, tile_qkv, True, s_qkv, land_qkv, own_qkv, st_row, wide_row, chips, sems_row)

    at_f1, at_gain = 3 * hcols, 3 * hcols + units + width
    at_beta = at_gain + width
    vec[...] = jnp.zeros_like(vec)
    vec[:, at_f1:at_gain] = sums[...]

    load_g.wait()
    load_act.wait()
    sc_f2.run()
    load_att = load(att_t, att_v, 1)
    load_qkv.wait()
    load_att_grad.wait()
    load_att.wait()
    sc_o.run()
    load_wqkv = load(gqkv, wqkv_v, 1)
    if count > 2:
        fold_out.pump(1, fetched, rows)

    qb = tile_of(length, QBLOCK)
    pairs = hcols // LANES
    row_segs = seg_row[...].astype(F32)

    def key_of(lo, hi):
        seg = seg_col[lo:hi, 0:1]
        return jnp.where(seg == 0.0, -1.0, seg)

    def turn_back(y, at):
        return y * table_c[at, :] - swapped(y) * table_s[at, :]

    def attend(pair, _):
        q_cols = aligned(pair, LANES)
        k_cols, v_cols = aligned(pairs + pair, LANES), aligned(2 * pairs + pair, LANES)
        lane = lax.broadcasted_iota(jnp.int32, (1, LANES), 1)
        dk_acc[...] = jnp.zeros_like(dk_acc)
        dv_acc[...] = jnp.zeros_like(dv_acc)
        k_t[...] = qkv[:, k_cols].T
        for b in range(length // qb):
            here, reach = slice(b * qb, (b + 1) * qb), (b + 1) * qb
            before = b * qb
            q2, g2 = qkv[here, q_cols], att_grad[here, q_cols]
            ki = lax.broadcasted_iota(jnp.int32, (qb, qb), 0)
            qi = lax.broadcasted_iota(jnp.int32, (qb, qb), 1)
            seen_here = jnp.logical_or(
                jnp.logical_and(key_of(before, reach) == row_segs[:, here], ki <= qi), ki == qi
            )
            dq_t = []
            for h in range(2):
                mine = (lane // HEAD_DIM) == h
                qh, gh = jnp.where(mine, q2, BF16(0)), jnp.where(mine, g2, BF16(0))
                stat = lse[pl.ds(2 * pair + h, 1), here]
                spans = ([(0, before)] if before else []) + [(before, reach)]
                probs, grads = [], []
                delta = jnp.zeros((1, qb), F32)
                for lo, hi in spans:
                    seen = seen_here if lo == before else key_of(lo, hi) == row_segs[:, here]
                    p = jnp.exp(jnp.where(seen, dot_nt(qkv[lo:hi, k_cols], qh), NEGATIVE) - stat)
                    pg = dot_nt(qkv[lo:hi, v_cols], gh)
                    delta = delta + jnp.sum(p * pg, axis=0, keepdims=True)
                    probs.append(p)
                    grads.append(pg)
                acc = jnp.zeros((HEAD_DIM, qb), F32)
                for (lo, hi), p, pg in zip(spans, probs, grads):
                    sg = (p * (pg - delta)).astype(BF16)
                    dv_acc[lo:hi, :] += dot_nn(p.astype(BF16), gh)
                    dk_acc[lo:hi, :] += dot_nn(sg, qh)
                    acc = acc + dot_nn(k_t[h * HEAD_DIM : (h + 1) * HEAD_DIM, lo:hi], sg)
                dq_t.append(acc)
            dq = jnp.concatenate(dq_t, axis=0).T * HEAD_DIM**-0.5
            qkv[here, q_cols] = turn_back(dq, here).astype(BF16)
        for b in range(length // qb):
            here = slice(b * qb, (b + 1) * qb)
            qkv[here, k_cols] = turn_back(dk_acc[here, :], here).astype(BF16)
            qkv[here, v_cols] = dv_acc[here, :].astype(BF16)
        for cols in (q_cols, k_cols, v_cols):
            vec[:, cols] = jnp.sum(qkv[:, cols].astype(F32), axis=0, keepdims=True)
        return 0

    half_pairs = pairs // 2
    lax.fori_loop(0, half_pairs, attend, 0)
    for k in range(2, count - 1):
        fold_out.pump(k, fetched, rows)
    lax.fori_loop(half_pairs, pairs, attend, 0)
    load_pre.wait()
    load_f1.wait()
    load_wqkv.wait()

    def hidden_back(d):
        here = pl.ds(d * rows, rows)

        def body(i, _):
            cols_i = aligned(i, wt)
            g[here, cols_i] = (
                dot_nt(pre[here, :], f1_v[cols_i, :]) + dot_nt(qkv[here, :], wqkv_v[cols_i, :])
            ).astype(BF16)
            return 0

        lax.fori_loop(0, width // wt, body, 0)

    def set_out(d):
        if d > 0:
            fold_hid.first(True, last - d, rows_of(g, d))
        if d < last:
            fold_hid.first(False, d, rows_of(g, d))

    dests = list(dict.fromkeys(d for both in zip(range(last, -1, -1), range(count)) for d in both))
    for d in dests[:2]:
        hidden_back(d)

    fold_out.arrive()
    load_x = pltpu.make_async_copy(x_in, tmp.at[0], tmp_sem.at[0])
    load_x.start()
    load_own = pltpu.make_async_copy(rows_of(part_in, z), tmp.at[1], tmp_sem.at[1])
    load_own.start()
    load_x.wait()
    load_own.wait()

    def finish_output(i, _):
        part = aligned(i, 32)
        y = fold_out.total(tmp[1, part, :].astype(F32), part)
        tmp[1, part, :] = (tmp[0, part, :].astype(F32) + y + out_bias[...]).astype(BF16)
        return 0

    lax.fori_loop(0, rows // 32, finish_output, 0)
    save_out = pltpu.make_async_copy(tmp.at[1], block_out, out_sem)
    save_out.start()
    fold_out.finish()

    @pl.when(z > 0)
    def _():
        pl.semaphore_signal(free_up, inc=1, device_id=(dp, z - 1), device_id_type=MESH)

    @pl.when(z < last)
    def _():
        pl.semaphore_signal(free_dn, inc=1, device_id=(dp, z + 1), device_id_type=MESH)

    @pl.when(z < last)
    def _():
        pl.semaphore_wait(free_up, 1)

    @pl.when(z > 0)
    def _():
        pl.semaphore_wait(free_dn, 1)

    for d in dests[:2]:
        set_out(d)
    run_rows(sc_f1)
    for d in dests[2:]:
        hidden_back(d)
        set_out(d)
    if count > 2:
        fold_hid.pump(1, lambda up, d: rows_of(g, d), rows)
    save_out.wait()
    load_cot = pltpu.make_async_copy(rows_of(gcot, z), tmp.at[1], tmp_sem.at[1])
    load_cot.start()
    run_rows(sc_qkv)
    for k in range(2, count - 1):
        fold_hid.pump(k, lambda up, d: rows_of(g, d), rows)
    fold_hid.arrive()
    load_cot.wait()

    step_rows = 32

    def ig_copy(i, slot):
        return pltpu.make_async_copy(ig_stage.at[slot], input_grad.at[aligned(i, step_rows), :], ig_sem.at[slot])

    def norm_back(i, _):
        part = aligned(i, step_rows)
        slot = lax.rem(i, 2)
        inputs = tmp[0, part, :].astype(F32)
        center = inputs - jnp.mean(inputs, axis=-1, keepdims=True)
        inverse = lax.rsqrt(jnp.mean(center * center, axis=-1, keepdims=True) + EPSILON)
        normed = center * inverse
        own = g[pl.ds(pl.multiple_of(z * rows + i * step_rows, step_rows), step_rows), :].astype(F32)
        y = fold_hid.total(own, part)
        vec[:, at_gain : at_gain + width] += jnp.sum(y * normed, axis=0, keepdims=True)
        vec[:, at_beta : at_beta + width] += jnp.sum(y, axis=0, keepdims=True)
        scaled = y * gain[...]
        result = tmp[1, part, :].astype(F32) + inverse * (
            scaled
            - jnp.mean(scaled, axis=-1, keepdims=True)
            - normed * jnp.mean(scaled * normed, axis=-1, keepdims=True)
        )

        @pl.when(i >= 2)
        def _():
            ig_copy(i, slot).wait()

        ig_stage[slot] = result
        ig_copy(i, slot).start()
        return 0

    steps = rows // step_rows
    lax.fori_loop(0, steps, norm_back, 0)

    to_pair = pltpu.make_async_remote_copy(
        src_ref=vec, dst_ref=vec_pair, send_sem=v_ps, recv_sem=v_pr,
        device_id=(chip * 2 + 1 - core, z), device_id_type=MESH,
    )
    to_pair.start()
    for i in range(max(steps - 2, 0), steps):
        ig_copy(i, i % 2).wait()
    to_pair.wait()
    vec_chip[chip] = vec[...] + vec_pair[...]

    def chip_copy(r, slot):
        return pltpu.make_async_remote_copy(
            src_ref=vec_chip.at[chip], dst_ref=vec_chip.at[slot], send_sem=v_cs.at[r - 1], recv_sem=v_cr.at[r - 1],
            device_id=(flip(chip, r) * 2 + core, z), device_id_type=MESH,
        )

    for r in range(1, chips):
        chip_copy(r, chip).start()
    for r in range(1, chips):
        chip_copy(r, flip(chip, r)).wait_recv()
    total = vec_chip[0]
    for c in range(1, chips):
        total = total + vec_chip[c]
    vec_out[:, 0:at_gain] = total[:, 0:at_gain]
    vec_z[z] = total[:, at_gain:]

    def z_copy(shift, slot):
        return pltpu.make_async_remote_copy(
            src_ref=vec_z.at[z], dst_ref=vec_z.at[slot], send_sem=v_zs.at[shift - 1], recv_sem=v_zr.at[shift - 1],
            device_id=(dp, lax.rem(z + shift, count)), device_id_type=MESH,
        )

    for shift in range(1, count):
        z_copy(shift, z).start()
    for shift in range(1, count):
        z_copy(shift, lax.rem(z + count - shift, count)).wait_recv()
    total = vec_z[0]
    for n in range(1, count):
        total = total + vec_z[n]
    vec_out[:, at_gain:] = total
    for r in range(1, chips):
        chip_copy(r, chip).wait_send()
    for shift in range(1, count):
        z_copy(shift, z).wait_send()
    fold_hid.finish()
    for s in (sc_f2, sc_f1, sc_o, sc_qkv):
        s.finish()


def run_backward(ndp, count, saved, x, lse, gain, out_bias, table_c, table_s, seg_row, seg_col, sums):
    chips = ndp // 2
    gqkv, gf1, gcot, hid_t, qkv, att_t = saved[:6]
    length, width = gcot.shape
    rows, hcols, units = length // count, att_t.shape[0], gf1.shape[1]
    part_w = width // ndp
    total = 3 * hcols + units + 3 * width
    anywhere = pl.BlockSpec(memory_space=pl.ANY)
    vmem = pl.BlockSpec(memory_space=pltpu.VMEM)
    low = lambda *shape: jax.ShapeDtypeStruct(shape, BF16)
    wide = lambda *shape: jax.ShapeDtypeStruct(shape, F32)
    outs = [
        low(rows, width), wide(rows, width), wide(1, total),
        wide(part_w, 3 * hcols), wide(part_w, units), wide(hcols, part_w), wide(units, part_w),
        low(chips - 1, part_w, 3 * hcols), low(chips - 1, part_w, units), low(chips - 1, hcols, part_w), low(chips - 1, units, part_w),
    ]
    v = lambda *shape: pltpu.VMEM(shape, BF16)
    w = lambda *shape: pltpu.VMEM(shape, F32)
    steps = max(count - 1, 1)
    dma = lambda *shape: pltpu.SemaphoreType.DMA(shape)
    row_tile = max(piece_of(units), piece_of(3 * hcols))
    col_tile = max(piece_of(units), piece_of(hcols))
    scratch = [
        v(length, width), v(length, units), v(width, units), v(max(units, width, hcols), max(3 * hcols, length)),
        v(length, 3 * hcols), v(length, hcols), w(length, LANES), w(length, LANES), v(LANES, length),
        v(4, part_w, length), v(2, rows, width),
        v(chips, part_w, 3 * hcols), v(chips, part_w, units), v(chips, hcols, part_w), v(chips, units, part_w),
        v(steps, rows, width), v(steps, rows, width),
        v(2, part_w, row_tile), v(2, col_tile, part_w), w(2, part_w, row_tile), w(2, col_tile, part_w),
        w(2, 32, width), w(1, total), w(1, total), w(chips, 1, total), w(count, 1, 2 * width),
        dma(6), dma(4), dma(2), pltpu.SemaphoreType.DMA, dma(2), dma(2), dma(2),
        dma(4, chips), dma(4, chips - 1), dma(4, chips - 1), dma(2), dma(2),
        *[dma(steps) for _ in range(8)], pltpu.SemaphoreType.REGULAR, pltpu.SemaphoreType.REGULAR,
        pltpu.SemaphoreType.DMA, pltpu.SemaphoreType.DMA, dma(chips - 1), dma(chips - 1), dma(steps), dma(steps),
    ]
    return pl.pallas_call(
        functools.partial(backward_kernel, chips, count),
        out_shape=outs,
        in_specs=[anywhere] * 11 + [vmem] * 8,
        out_specs=[anywhere, anywhere, vmem] + [anywhere] * 8,
        scratch_shapes=scratch,
        compiler_params=pltpu.CompilerParams(
            collective_id=1, has_side_effects=True, vmem_limit_bytes=VMEM_LIMIT
        ),
        name="backward_scatter",
    )(*saved, x, lse, gain, out_bias, table_c, table_s, seg_row, seg_col, sums)


def on_device(
    ndp, count,
    block_input, segment_ids, out_cotangent, norm_gain, norm_bias, query_weight, key_weight, value_weight,
    query_bias, key_bias, value_bias, out_weight, fc1_weight, fc1_bias, fc2_weight, output_bias,
):
    x = block_input[0]
    cot = out_cotangent[0]
    width = x.shape[1]
    half_rot = ROT // 2
    frequency = 10000.0 ** (-2.0 * (jnp.arange(LANES, dtype=jnp.int32) % half_rot).astype(F32) / ROT)
    bqkv = jnp.concatenate([query_bias, key_bias, value_bias])[None, :]
    gain, seg_row = norm_gain[None, :], segment_ids
    (gqkv, gf1, gcot, hid_t, qkv, att_t, lse, act_t, pre, part, att_grad, table_c, table_s, seg_col, sums) = run_forward(
        ndp, count, x, gain, norm_bias[None, :], bqkv, fc1_bias[None, :], seg_row, frequency[None, :],
        query_weight, key_weight, value_weight, fc1_weight, out_weight, fc2_weight, cot,
    )
    (block_output, input_grad, vec, own_qkv, own_f1, own_o, own_f2, land_qkv, land_f1, land_o, land_f2) = run_backward(
        ndp, count, (gqkv, gf1, gcot, hid_t, qkv, att_t, act_t, pre, part, att_grad), x, lse,
        gain, output_bias[None, :], table_c, table_s, seg_row, seg_col, sums,
    )
    hcols, units = out_weight.shape[0], fc2_weight.shape[0]

    def summed(own, landed):
        for n in range(landed.shape[0]):
            own = own + landed[n].astype(F32)
        return own

    def third(i):
        cols = slice(i * hcols, (i + 1) * hcols)
        return summed(own_qkv[:, cols], land_qkv[:, :, cols])

    sizes = (hcols, hcols, hcols, units, width, width, width)
    pieces, at = [], 0
    for size in sizes:
        pieces.append(vec[0, at : at + size])
        at += size
    qb, kb, vb, f1b, ob, gain_grad, beta_grad = pieces
    return (
        block_output[None], input_grad[None], gain_grad, beta_grad,
        third(0), third(1), third(2), qb, kb, vb,
        summed(own_o, land_o), summed(own_f1, land_f1), f1b, summed(own_f2, land_f2), ob,
    )


def solution(mesh):
    tokens, vector, split = P("dp", "branch", None), P(), P("branch")
    rows_first, cols_first = P("dp", "branch"), P("branch", "dp")
    in_specs = (
        tokens, P("dp", None), tokens, vector, vector, rows_first, rows_first, rows_first,
        split, split, split, cols_first, rows_first, split, cols_first, vector,
    )
    out_specs = (
        tokens, tokens, vector, vector, rows_first, rows_first, rows_first, split, split, split,
        cols_first, rows_first, split, cols_first, vector,
    )
    return jax.shard_map(
        functools.partial(on_device, mesh.shape["dp"], mesh.shape["branch"]),
        mesh=mesh, in_specs=in_specs, out_specs=out_specs, check_vma=False,
    )
```

profile of v0, /device:TPU:0, one launch (start us, length us, event | category | flops | bytes accessed | tf_op | source)
XLA Modules:
  0.0 383.3 jit_solution(8496876276877934571)
XLA Ops:
  0.6 0.5 fusion.2.frequency
  1.2 0.7 pad_maximum_fusion
  1.9 0.6 broadcast_in_dim.24.bqkv
  2.5 156.0 %gather_forward.1 = (bf16[2048,1536]{1,0:T(8,128)(2,1)}, bf16[2048,2048]{1,0:T(8,128)(2,1)}, bf16[1024,2048]{1,0:T(8,128)(2,1)}, bf16[2048,1024]{1,0:T(8,128)(2,...) custom-call(bf16[256,2048]{1,0:T(8,128)(2,1)} %bitcast.69, ...), custom_call_target="tpu_custom_call" | custom-call | tf_op jit(solution)/shard_map/gather_forward/pallas_call | solution.py:546
  158.5 207.2 %backward_scatter.1 = (bf16[256,2048]{1,0:T(8,128)(2,1)}, f32[256,2048]{1,0:T(8,128)}, f32[1,9728]{1,0:T(1,128)}, f32[256,1536]{1,0:T(8,128)}, f32[256,2048]{1,0...) custom-call(bf16[2048,1536]{1,0:T(8,128)(2,1)} %get-tuple-element.41, ...), custom_call_target="tpu_custom_call" | custom-call | tf_op jit(solution)/shard_map/backward_scatter/pallas_call | solution.py:1142
  365.7 0.0 copy-start.5
  365.7 1.4 fusion.4
  367.1 1.4 fusion.3
  368.5 2.2 convert_add_fusion.6
  370.7 0.0 copy-done.5
  370.7 0.0 copy-start.1
  370.7 0.0 copy-start.3
  370.7 3.2 convert_add_fusion.9
  373.9 0.0 copy-done.1
  373.9 0.6 copy-done.3
  374.5 0.0 copy-start
  374.5 0.0 copy-start.2
  374.5 1.9 convert_add_fusion.3
  376.4 0.7 copy-done
  377.1 0.7 copy-done.2
  377.8 0.0 copy-start.6
  377.8 1.7 convert_add_fusion
  379.5 0.0 copy-done.6
  379.5 0.0 copy-start.4
  379.5 1.0 copy.33
  380.5 1.0 copy-done.4
  381.5 1.3 copy.34
Async XLA Ops:
  365.7 4.9 %copy-start.5 = (f32[256,1536]{1,0:T(8,128)S(1)}, f32[256,1536]{1,0:T(8,128)}, u32[]{:S(2)}) copy-start(f32[256,1536]{1,0:T(8,128)} %get-tuple-element.59) | copy-start | bytes 4718596
  370.7 3.2 copy-start.1
  370.7 3.8 %copy-start.3 = (f32[256,2048]{1,0:T(8,128)S(1)}, f32[256,2048]{1,0:T(8,128)}, u32[]{:S(2)}) copy-start(f32[256,2048]{1,0:T(8,128)} %get-tuple-element.63) | copy-start | bytes 6291460
  374.5 2.6 copy-start
  374.5 3.3 copy-start.2
  377.8 1.7 copy-start.6
  379.5 2.0 copy-start.4
where the time goes:
time: 391 us; the launch traced here: 383 us
  Pallas kernels  363 us (93%)
  other arithmetic  10.3 us (3%)
  local copies, waits for them, and re-layouts  8.63 us (2%)
    pallas_call x1, Pallas kernels, run_backward(): pl.pallas_call(functools.partial(backward_kernel, chips, count), out_shap...  207 us
    pallas_call x1, Pallas kernels, run_forward(): pl.pallas_call(functools.partial(forward_kernel, chips, count), out_shape...  156 us
    add x4, other arithmetic, summed(): own = own + landed[n].astype(F32)  9.03 us

commit v1 on v0

v1 whole, which is shorter than its diff:
```python
import functools

import jax
import jax.numpy as jnp
from jax import lax
from jax.experimental import pallas as pl
from jax.experimental.pallas import tpu as pltpu
from jax.sharding import PartitionSpec as P

HEAD_DIM = 64
ROT = 32
EPSILON = 1e-05
NEGATIVE = -1e30
LANES = 128
TILE = 512
QBLOCK = 256
MESH = pl.DeviceIdType.MESH
BF16 = jnp.bfloat16
F32 = jnp.float32
GELU_C = 0.7978845608028654
GELU_A = 0.044715
VMEM_LIMIT = 63 * 1024 * 1024 + 832 * 1024


def flip(index, bits):
    out = index
    bit = 1
    while bit <= bits:
        if bits & bit:
            out = out + bit * (1 - 2 * lax.rem(lax.div(index, bit), 2))
        bit *= 2
    return out


def dot_nn(left, right):
    return jnp.dot(left, right, preferred_element_type=F32)


def dot_nt(left, right):
    return lax.dot_general(left, right, (((1,), (1,)), ((), ())), preferred_element_type=F32)


def tile_of(extent, most=TILE):
    return min(most, extent)


def aligned(index, step):
    return pl.ds(pl.multiple_of(index * step, step), step)


class Chain:
    def __init__(self, own_src, buf, rows, count, sems, dp):
        self.own_src, self.buf, self.rows, self.count = own_src, buf, rows, count
        self.sems, self.dp = sems, dp
        self.z = lax.axis_index("branch")

    def block(self, slot):
        return self.buf.at[aligned(slot, self.rows), :]

    def copy(self, up, step, slot, src=None):
        send, recv = self.sems[0 if up else 2], self.sems[1 if up else 3]
        return pltpu.make_async_remote_copy(
            src_ref=self.block(slot) if src is None else src,
            dst_ref=self.block(slot),
            send_sem=send.at[step],
            recv_sem=recv.at[step],
            device_id=(self.dp, self.z + 1 if up else self.z - 1),
            device_id_type=MESH,
        )

    def sends(self, up, step):
        z, last = self.z, self.count - 1
        if up:
            return jnp.logical_and(z >= step, z < last)
        return jnp.logical_and(z + step <= last, z > 0)

    def sent_slot(self, up, step):
        return self.z - step if up else self.z + step

    def start(self):
        for up in (False, True):

            @pl.when(self.sends(up, 0))
            def _(up=up):
                self.copy(up, 0, self.z, self.own_src).start()

    def pump(self, step):
        for up in (False, True):

            @pl.when(self.sends(up, step))
            def _(up=up):
                slot = self.sent_slot(up, step)
                self.copy(up, step - 1, slot).wait_recv()
                self.copy(up, step, slot).start()

    def by_distance(self, first, end, work):
        def visit(i, _):
            far = lax.div(i + 1, 2)
            above = lax.rem(i, 2) == 0
            slot = self.z + jnp.where(above, far, -far)

            @pl.when(jnp.logical_and(slot >= 0, slot <= self.count - 1))
            def _():
                for up in (False, True):
                    mine = jnp.logical_and(far > 0, above if not up else jnp.logical_not(above))

                    @pl.when(jnp.logical_and(mine, jnp.logical_not(self.sends(up, far))))
                    def _(up=up):
                        self.copy(up, far - 1, slot).wait_recv()

                work(slot)

            return 0

        lax.fori_loop(first, end, visit, 0)

    def finish(self):
        for step in range(self.count - 1):
            for up in (False, True):

                @pl.when(self.sends(up, step))
                def _(up=up, step=step):
                    self.copy(up, step, self.sent_slot(up, step), self.own_src if step == 0 else None).wait_send()


class Gather:
    def __init__(self, index, shard, full, by_rows, chips, sems):
        self.index, self.shard, self.full = index, shard, full
        self.by_rows, self.chips = by_rows, chips
        self.send, self.recv, self.relay_send, self.relay_recv, self.pair_send, self.pair_recv, self.own = sems
        dp = lax.axis_index("dp")
        self.z = lax.axis_index("branch")
        self.core = lax.rem(dp, 2)
        self.chip = lax.div(dp, 2)
        self.width = shard.shape[0 if by_rows else 1]
        self.relayed = chips == 4
        self.direct = (1, 2) if self.relayed else tuple(range(1, chips))

    def slot(self, dp):
        part = aligned(dp, self.width)
        return self.full.at[part, :] if self.by_rows else self.full.at[:, part]

    def half(self, dp, which):
        if self.by_rows:
            return self.full.at[aligned(2 * dp + which, self.width // 2), :]
        rows = self.shard.shape[0] // 2
        return self.full.at[pl.ds(which * rows, rows), aligned(dp, self.width)]

    def at(self, r, core):
        return flip(self.chip, r) * 2 + core

    def to_chip(self, r, landing):
        return pltpu.make_async_remote_copy(
            src_ref=self.shard,
            dst_ref=self.slot(landing),
            send_sem=self.send.at[self.index, r - 1],
            recv_sem=self.recv.at[self.index, r - 1],
            device_id=(self.at(r, self.core), self.z),
            device_id_type=MESH,
        )

    def relay(self, which, owner):
        return pltpu.make_async_remote_copy(
            src_ref=self.half(owner, which),
            dst_ref=self.half(owner, which),
            send_sem=self.relay_send.at[self.index, which],
            recv_sem=self.relay_recv.at[self.index, which],
            device_id=(self.at(2 - which, self.core), self.z),
            device_id_type=MESH,
        )

    def to_pair(self, r, landing):
        return pltpu.make_async_remote_copy(
            src_ref=self.shard if r == 0 else self.slot(self.at(r, self.core)),
            dst_ref=self.slot(landing),
            send_sem=self.pair_send.at[self.index, r],
            recv_sem=self.pair_recv.at[self.index, r],
            device_id=(self.chip * 2 + 1 - self.core, self.z),
            device_id_type=MESH,
        )

    def fetch(self):
        return pltpu.make_async_copy(self.shard, self.slot(self.at(0, self.core)), self.own.at[self.index])

    def start(self):
        for r in self.direct:
            self.to_chip(r, self.at(0, self.core)).start()

    def start_pair(self):
        self.to_pair(0, self.at(0, self.core)).start()
        self.fetch().start()

    def land(self):
        for r in self.direct:
            owner = self.at(r, self.core)
            self.to_chip(r, owner).wait_recv()
            if self.relayed:
                self.relay(r - 1, owner).start()
            self.to_pair(r, owner).start()

    def land_last(self):
        if self.relayed:
            owner = self.at(3, self.core)
            for which in range(2):
                self.relay(which, owner).wait_recv()
            self.to_pair(3, owner).start()

    def arrive(self):
        self.fetch().wait()
        for r in range(self.chips):
            self.to_pair(r, self.at(r, 1 - self.core)).wait_recv()

    def finish(self):
        for r in self.direct:
            self.to_chip(r, self.at(0, self.core)).wait_send()
            if self.relayed:
                self.relay(r - 1, self.at(r, self.core)).wait_send()
        for r in range(self.chips):
            self.to_pair(r, self.at(r, self.core)).wait_send()


def greet(chips, count):
    dp, z = lax.axis_index("dp"), lax.axis_index("branch")
    core, chip = lax.rem(dp, 2), lax.div(dp, 2)
    barrier = pltpu.get_barrier_semaphore()
    for r in range(1, chips):
        pl.semaphore_signal(barrier, inc=1, device_id=(flip(chip, r) * 2 + core, z), device_id_type=MESH)
    pl.semaphore_signal(barrier, inc=1, device_id=(chip * 2 + 1 - core, z), device_id_type=MESH)
    for shift in range(1, count):
        pl.semaphore_signal(barrier, inc=1, device_id=(dp, lax.rem(z + shift, count)), device_id_type=MESH)
    pl.semaphore_wait(barrier, chips + count - 1)


def swapped(y):
    lane = lax.rem(lax.broadcasted_iota(jnp.int32, y.shape, 1), HEAD_DIM)
    return jnp.where(lane < ROT // 2, pltpu.roll(y, LANES - ROT // 2, 1), pltpu.roll(y, ROT // 2, 1))


class Fold:
    def __init__(self, bufs, sems, count, dp):
        self.bufs, self.sems, self.count, self.dp = bufs, sems, count, dp
        self.z = lax.axis_index("branch")

    def place(self, up):
        return self.z if up else self.count - 1 - self.z

    def dest(self, up, step):
        return self.count - 1 - step if up else step

    def hop(self, up, step, src=None):
        buf = self.bufs[0 if up else 1]
        send, recv = self.sems[0 if up else 2], self.sems[1 if up else 3]
        return pltpu.make_async_remote_copy(
            src_ref=buf.at[step] if src is None else src,
            dst_ref=buf.at[step],
            send_sem=send.at[step],
            recv_sem=recv.at[step],
            device_id=(self.dp, self.z + 1 if up else self.z - 1),
            device_id_type=MESH,
        )

    def first(self, up, step, src):
        @pl.when(self.place(up) == 0)
        def _():
            self.hop(up, step, src).start()

    def pump(self, k, own_block, rows):
        for up in (False, True):
            place = self.place(up)

            @pl.when(jnp.logical_and(place >= 1, place <= k))
            def _(up=up, place=place):
                step = k - place
                own = own_block(up, self.dest(up, step))
                self.hop(up, step).wait_recv()
                buf = self.bufs[0 if up else 1]

                def add(i, _):
                    part = aligned(i, 32)
                    buf[step, part, :] = (buf[step, part, :].astype(F32) + own[part, :].astype(F32)).astype(BF16)
                    return 0

                lax.fori_loop(0, rows // 32, add, 0)
                self.hop(up, step).start()

    def last_step(self, up):
        return jnp.clip(self.count - 1 - self.place(up), 0, self.count - 2)

    def arrive(self):
        for up in (False, True):

            @pl.when(self.place(up) >= 1)
            def _(up=up):
                self.hop(up, self.last_step(up)).wait_recv()

    def total(self, own, part):
        out = own
        for up in (False, True):
            got = self.bufs[0 if up else 1][self.last_step(up), part, :].astype(F32)
            out = out + jnp.where(self.place(up) >= 1, got, 0.0)
        return out

    def finish(self):
        for step in range(self.count - 1):
            for up in (False, True):

                @pl.when(self.place(up) + step <= self.count - 2)
                def _(up=up, step=step):
                    self.hop(up, step).wait_send()


class Scatter:
    def __init__(self, index, block, tile, rows_first, base, size, landing, own_out, stage, wide, chips, sems):
        self.index, self.block, self.tile, self.rows_first = index, block, tile, rows_first
        self.base, self.size, self.landing, self.own_out = base, size, landing, own_out
        self.stage, self.wide = stage, wide
        self.chips = chips
        self.st_sem, self.pair_recv, self.send, self.recv, self.wide_sem = sems
        dp = lax.axis_index("dp")
        self.z = lax.axis_index("branch")
        self.core, self.chip = lax.rem(dp, 2), lax.div(dp, 2)
        self.tiles = size[1 if rows_first else 0] // tile
        self.height = size[0] if rows_first else tile
        self.breadth = tile if rows_first else size[1]
        self.order = [*range(1, chips), 0]

    def slot(self, r):
        high, wide = self.size
        if self.rows_first:
            return self.base.at[r * high : (r + 1) * high, 0:wide]
        return self.base.at[0:high, r * wide : (r + 1) * wide]

    def slot_part(self, r, i):
        high, wide = self.size
        at = aligned(i, self.tile)
        return (pl.ds(r * high, high), at) if self.rows_first else (at, pl.ds(r * wide, wide))

    def part(self, ref, i):
        at = aligned(i, self.tile)
        return ref.at[:, at] if self.rows_first else ref.at[at, :]

    def view(self, ref, slot):
        return ref.at[slot, pl.ds(0, self.height), pl.ds(0, self.breadth)]

    def to_pair(self, r, i, slot):
        return pltpu.make_async_remote_copy(
            src_ref=self.view(self.stage, slot),
            dst_ref=self.base.at[self.slot_part(r, i)],
            send_sem=self.st_sem.at[slot],
            recv_sem=self.pair_recv.at[self.index, r],
            device_id=(self.chip * 2 + 1 - self.core, self.z),
            device_id_type=MESH,
        )

    def from_pair(self, r):
        return pltpu.make_async_remote_copy(
            src_ref=self.slot(r),
            dst_ref=self.slot(r),
            send_sem=self.st_sem.at[0],
            recv_sem=self.pair_recv.at[self.index, r],
            device_id=(self.chip * 2 + 1 - self.core, self.z),
            device_id_type=MESH,
        )

    def to_owner(self, r):
        return pltpu.make_async_remote_copy(
            src_ref=self.slot(r),
            dst_ref=self.landing.at[r - 1],
            send_sem=self.send.at[self.index, r - 1],
            recv_sem=self.recv.at[self.index, r - 1],
            device_id=(flip(self.chip, r) * 2 + self.core, self.z),
            device_id_type=MESH,
        )

    def to_out(self, i):
        source = self.wide.at[0 : self.height, 0 : self.breadth]
        return pltpu.make_async_copy(source, self.part(self.own_out, i), self.wide_sem)

    def partners(self, n):
        r = self.order[n]
        owner = flip(self.chip, r) * 2 + 1 - self.core

        def body(i, _):
            slot = lax.rem(n * self.tiles + i, 2)
            y = self.block(owner, i)
            if n * self.tiles >= 2:
                self.to_pair(r, i, slot).wait_send()
            else:

                @pl.when(n * self.tiles + i >= 2)
                def _():
                    self.to_pair(r, i, slot).wait_send()

            self.stage[slot, 0 : self.height, 0 : self.breadth] = y.astype(BF16)
            self.to_pair(r, i, slot).start()
            return 0

        lax.fori_loop(0, self.tiles, body, 0)

    def own(self, n):
        r = self.order[n]
        owner = flip(self.chip, r) * 2 + self.core
        self.from_pair(r).wait_recv()

        def body(i, _):
            y = self.block(owner, i)
            at = self.slot_part(r, i)
            y = y + self.base[at].astype(F32)
            if r:
                self.base[at] = y.astype(BF16)
            else:
                @pl.when(i >= 1)
                def _():
                    self.to_out(i).wait()

                self.wide[0 : self.height, 0 : self.breadth] = y
                self.to_out(i).start()
            return 0

        lax.fori_loop(0, self.tiles, body, 0)
        if r:
            self.to_owner(r).start()
        else:
            self.to_out(self.tiles - 1).wait()

    def run(self, before=lambda n: None):
        for n in range(self.chips):
            before(n)
            self.partners(n)
            if n:
                self.own(n - 1)
        self.own(self.chips - 1)
        self.drain()

    def drain(self):
        total = self.chips * self.tiles
        for i in range(max(total - 2, 0), total):
            self.to_pair(0, 0, i % 2).wait_send()

    def sent(self):
        for r in range(1, self.chips):
            self.to_owner(r).wait_send()

    def finish(self):
        for r in range(1, self.chips):
            self.to_owner(r).wait_recv()


def piece_of(extent):
    return next(n for n in (512, 256, 128) if extent % n == 0)


def block_kernel(
    chips, count,
    x, gain, beta, bqkv, bf1, out_bias, seg_row, frequency, wq, wk, wv, wf1, wo, wf2, cot,
    block_out, input_grad, vec_out, own_qkv, own_f1, own_o, own_f2, land_qkv, land_f1, land_o, land_f2, hid_t, act_t,
    hid, vqkv, vf1, vf2, vo, qkv, att, att_t, lse, act, dg, g, stage, tab_c, tab_s, segs,
    dk_acc, dv_acc, k_t, up_buf, dn_buf, wide_row, wide_col, ig_stage, vec, vec_pair, vec_chip, vec_z,
    w_send, w_recv, r_send, r_recv, p_send, p_recv, own_sem,
    h_us, h_ur, h_ds, h_dr, c_us, c_ur, c_ds, c_dr, cot_sem, st_sem,
    act_sem, hid_sem, out_sem, ig_sem, st_row_sem, st_col_sem, pair_recv, x_send, x_recv, wide_row_sem, wide_col_sem,
    zo_us, zo_ur, zo_ds, zo_dr, zh_us, zh_ur, zh_ds, zh_dr, free_up, free_dn, pair_free, hid_free,
    v_ps, v_pr, v_cs, v_cr, v_zs, v_zr,
):
    z = lax.axis_index("branch")
    dp = lax.axis_index("dp")
    core, chip = lax.rem(dp, 2), lax.div(dp, 2)
    rows, width = x.shape
    length = rows * count
    hcols = wo.shape[0]
    units = wf2.shape[0]
    part_w = width // (2 * chips)
    last = count - 1
    sems = (w_send, w_recv, r_send, r_recv, p_send, p_recv, own_sem)
    g_qkv = [
        Gather(n, w, vqkv.at[:, n * hcols : (n + 1) * hcols], True, chips, sems) for n, w in enumerate((wq, wk, wv))
    ]
    g_f1 = Gather(3, wf1, vf1, True, chips, sems)
    g_o = Gather(4, wo, vo, False, chips, sems)
    g_f2 = Gather(5, wf2, vf2, False, chips, sems)
    h_chain = Chain(hid.at[aligned(z, rows), :], hid, rows, count, (h_us, h_ur, h_ds, h_dr), dp)
    c_chain = Chain(cot, g, rows, count, (c_us, c_ur, c_ds, c_dr), dp)
    part = hid
    act_v = vf2.at[0:units, width // 2 : width // 2 + length]

    def rows_of(ref, d):
        return ref.at[aligned(d, rows), :]

    fold_out = Fold((up_buf, dn_buf), (zo_us, zo_ur, zo_ds, zo_dr), count, dp)
    fold_hid = Fold((up_buf, dn_buf), (zh_us, zh_ur, zh_ds, zh_dr), count, dp)

    at_f1, at_ob, at_gain = 3 * hcols, 3 * hcols + units, 3 * hcols + units + width
    at_beta = at_gain + width

    def hand_over(free):
        pl.semaphore_signal(free, inc=1, device_id=(chip * 2 + 1 - core, z), device_id_type=MESH)
        pl.semaphore_wait(free, 1)

    sems_row = (st_row_sem, pair_recv, x_send, x_recv, wide_row_sem)
    sems_col = (st_col_sem, pair_recv, x_send, x_recv, wide_col_sem)
    tile_f2, tile_o = piece_of(units), piece_of(hcols)
    tile_f1, tile_qkv = piece_of(units), piece_of(3 * hcols)

    def f2_block(owner, i):
        return dot_nn(act_v[aligned(i, tile_f2), :], g[:, aligned(owner, part_w)])

    def o_block(owner, i):
        return dot_nn(att_t[aligned(i, tile_o), :], g[:, aligned(owner, part_w)])

    def hid_part(n):
        return vo.at[(n % 2) * part_w : (n % 2 + 1) * part_w, width // 2 : width // 2 + length]

    def hid_copy(n, owner):
        return pltpu.make_async_copy(hid_t.at[aligned(owner, part_w), :], hid_part(n), hid_sem.at[n % 2])

    state = {}

    def f1_block(owner, i):
        return dot_nn(hid_part(state["at"])[...], dg[:, aligned(i, tile_f1)])

    def qkv_block(owner, i):
        return dot_nn(hid_part(state["at"])[...], qkv[:, aligned(i, tile_qkv)])

    def run_rows(scatter, between=None):
        turns = [(True, 0)]
        for n in range(1, chips):
            turns += [(True, n), (False, n - 1)]
        turns.append((False, chips - 1))
        owners = [flip(chip, scatter.order[n]) * 2 + (1 - core if pair else core) for pair, n in turns]
        hid_copy(0, owners[0]).start()
        for i, (pair, n) in enumerate(turns):
            if i + 1 < len(turns):
                hid_copy(i + 1, owners[i + 1]).start()
            hid_copy(i, owners[i]).wait()
            state["at"] = i
            (scatter.partners if pair else scatter.own)(n)
            if between is not None and i == len(turns) // 2:
                between()
        scatter.drain()

    sc_f2 = Scatter(0, f2_block, tile_f2, False, vf2, (units, part_w), land_f2, own_f2, stage, wide_col, chips, sems_col)
    sc_f1 = Scatter(1, f1_block, tile_f1, True, act, (part_w, units), land_f1, own_f1, stage, wide_row, chips, sems_row)
    sc_o = Scatter(2, o_block, tile_o, False, vo, (hcols, part_w), land_o, own_o, stage, wide_col, chips, sems_col)
    sc_qkv = Scatter(3, qkv_block, tile_qkv, True, hid, (part_w, 3 * hcols), land_qkv, own_qkv, stage, wide_row, chips, sems_row)

    greet(chips, count)
    for gw in (*g_qkv, g_f1):
        gw.start()
    for gw in (*g_qkv, g_f1, g_o, g_f2):
        gw.start_pair()
    fetch_cot = pltpu.make_async_copy(cot, g.at[aligned(z, rows), :], cot_sem)
    fetch_cot.start()

    step_rows = 32

    def norm(i, _):
        part_rows = aligned(i, step_rows)
        inputs = x[part_rows, :].astype(F32)
        center = inputs - jnp.mean(inputs, axis=-1, keepdims=True)
        inverse = lax.rsqrt(jnp.mean(center * center, axis=-1, keepdims=True) + EPSILON)
        where = pl.ds(pl.multiple_of(z * rows + i * step_rows, step_rows), step_rows)
        hid[where, :] = (center * inverse * gain[...] + beta[...]).astype(BF16)
        return 0

    lax.fori_loop(0, rows // step_rows, norm, 0)
    h_chain.start()
    vec[...] = jnp.zeros_like(vec)

    row_segs = seg_row[...].astype(F32)
    places = lax.broadcasted_iota(jnp.int32, (1, length), 1).astype(F32)
    firsts = [
        jnp.min(jnp.where(row_segs == float(value), places, float(length)), axis=1, keepdims=True)
        for value in range(4)
    ]
    for c in range(length // LANES):
        here = slice(c * LANES, (c + 1) * LANES)
        seg = jnp.broadcast_to(row_segs[:, here], (LANES, LANES)).T
        segs[here, :] = seg.astype(BF16)
        start = jnp.zeros((LANES, LANES), F32)
        for value in range(4):
            start = jnp.where(seg == float(value), firsts[value], start)
        place = (lax.broadcasted_iota(jnp.int32, (LANES, LANES), 0) + c * LANES).astype(F32)
        angle = (place - start) * frequency[...]
        lane = lax.rem(lax.broadcasted_iota(jnp.int32, (LANES, LANES), 1), HEAD_DIM)
        sine = jnp.where(lane < ROT, jnp.sin(angle), 0.0)
        tab_c[here, :] = jnp.where(lane < ROT, jnp.cos(angle), 1.0)
        tab_s[here, :] = jnp.where(lane < ROT // 2, -sine, sine)
    key_row = jnp.where(row_segs == 0.0, -1.0, row_segs)

    for gw in g_qkv:
        gw.land()
    if count > 2:
        h_chain.pump(1)
    g_f1.land()
    for gw in (g_o, g_f2):
        gw.start()
    for s in range(2, count - 1):
        h_chain.pump(s)
    c_chain.start()
    for gw in g_qkv:
        gw.land_last()
    for gw in g_qkv:
        gw.arrive()

    ht, wt = tile_of(hcols), tile_of(width)

    def turn_copy(slot, j, cols_i):
        return pltpu.make_async_copy(
            stage.at[slot, pl.ds(0, wt), pl.ds(0, rows)], hid_t.at[cols_i, aligned(j, rows)], st_sem.at[slot]
        )

    def project(j):
        rows_j = aligned(j, rows)
        for which in range(3):
            for c in range(hcols // ht):
                at = which * hcols + c * ht
                y = dot_nn(hid[rows_j, :], vqkv[:, at : at + ht]) + bqkv[:, at : at + ht]
                for piece in range(ht // LANES):
                    part_y = y[:, piece * LANES : (piece + 1) * LANES]
                    if which < 2:
                        part_y = part_y * tab_c[rows_j, :] + swapped(part_y) * tab_s[rows_j, :]
                    low = part_y.astype(BF16)
                    if which == 0:
                        low = low * BF16(HEAD_DIM**-0.5)
                    qkv[rows_j, at + piece * LANES : at + (piece + 1) * LANES] = low

        def turn(i, _):
            cols_i, slot = aligned(i, wt), lax.rem(i, 2)

            @pl.when(i >= 2)
            def _():
                turn_copy(slot, j, cols_i).wait()

            stage[slot, 0:wt, 0:rows] = hid[rows_j, cols_i].T
            turn_copy(slot, j, cols_i).start()
            return 0

        n_turn = width // wt
        lax.fori_loop(0, n_turn, turn, 0)
        for i in range(max(n_turn - 2, 0), n_turn):
            turn_copy(i % 2, j, pl.ds(0, wt)).wait()

    h_chain.by_distance(0, 2 * count - 3, project)
    g_o.land()
    h_chain.by_distance(2 * count - 3, 2 * count - 1, project)
    g_f2.land()
    if count > 2:
        c_chain.pump(1)

    qb = tile_of(length, QBLOCK)
    pairs = hcols // LANES

    def attend(pair, _):
        cols = aligned(pair, LANES)
        k_cols, v_cols = aligned(pairs + pair, LANES), aligned(2 * pairs + pair, LANES)
        lane = lax.broadcasted_iota(jnp.int32, (1, LANES), 1)
        for b in range(length // qb):
            here = slice(b * qb, (b + 1) * qb)
            before = b * qb
            q2 = qkv[here, cols]
            seg_q = segs[here, 0:1].astype(F32)
            ki = lax.broadcasted_iota(jnp.int32, (qb, qb), 1)
            qi = lax.broadcasted_iota(jnp.int32, (qb, qb), 0)
            seen_here = jnp.logical_or(jnp.logical_and(seg_q == key_row[:, here], ki <= qi), ki == qi)
            out = jnp.zeros((qb, LANES), F32)
            stat = jnp.zeros((qb, LANES), F32)
            for h in range(2):
                mine = (lane // HEAD_DIM) == h
                qh = jnp.where(mine, q2, BF16(0))
                s_here = jnp.where(seen_here, dot_nt(qh, qkv[here, k_cols]), NEGATIVE)
                top = jnp.max(s_here, axis=-1, keepdims=True)
                if before:
                    s_before = jnp.where(
                        seg_q == key_row[:, :before], dot_nt(qh, qkv[:before, k_cols]), NEGATIVE
                    )
                    top = jnp.maximum(top, jnp.max(s_before, axis=-1, keepdims=True))
                e_here = jnp.exp(s_here - top)
                total = jnp.sum(e_here, axis=-1, keepdims=True)
                if before:
                    e_before = jnp.exp(s_before - top)
                    total = total + jnp.sum(e_before, axis=-1, keepdims=True)
                share = 1.0 / total
                o = dot_nn((e_here * share).astype(BF16), jnp.where(mine, qkv[here, v_cols], BF16(0)))
                if before:
                    o = o + dot_nn(
                        (e_before * share).astype(BF16), jnp.where(mine, qkv[:before, v_cols], BF16(0))
                    )
                out = out + o
                stat = jnp.where(mine, top + jnp.log(total), stat)
            att[here, cols] = out.astype(BF16)
            att_t[cols, here] = out.T.astype(BF16)
            turned = stat.T
            lse[pl.ds(2 * pair, 1), here] = turned[0:1, :]
            lse[pl.ds(2 * pair + 1, 1), here] = turned[HEAD_DIM : HEAD_DIM + 1, :]
        return 0

    half_pairs = pairs // 2
    lax.fori_loop(0, half_pairs, attend, 0)
    for s in range(2, count - 1):
        c_chain.pump(s)
    lax.fori_loop(half_pairs, pairs - 1, attend, 0)
    g_f1.land_last()
    lax.fori_loop(pairs - 1, pairs, attend, 0)
    g_f1.arrive()

    mt, ft = tile_of(length), tile_of(units)
    per_row = units // ft
    n_tiles = (length // mt) * per_row

    def staged(slot, rows_i, cols_i):
        return pltpu.make_async_copy(stage.at[slot, pl.ds(0, ft), :], act_t.at[cols_i, rows_i], st_sem.at[slot])

    def unit(i, _):
        rows_i, cols_i = aligned(lax.div(i, per_row), mt), aligned(lax.rem(i, per_row), ft)
        slot = lax.rem(i, 2)

        @pl.when(i >= 2)
        def _():
            staged(slot, rows_i, cols_i).wait()

        y = dot_nn(hid[rows_i, :], vf1[:, cols_i]) + bf1[:, cols_i]
        square = y * y
        t = jnp.tanh(GELU_C * (y + GELU_A * (y * square)))
        half = 0.5 * (1.0 + t)
        low = (y * half).astype(BF16)
        act[rows_i, cols_i] = low
        stage[slot, 0:ft, :] = low.T
        dg[rows_i, cols_i] = (
            half + 0.5 * y * (1.0 - t * t) * (GELU_C * (1.0 + 3.0 * GELU_A * square))
        ).astype(BF16)
        staged(slot, rows_i, cols_i).start()
        return 0

    half_tiles = n_tiles // 2
    lax.fori_loop(0, half_tiles, unit, 0)
    for gw in (g_o, g_f2):
        gw.land_last()
    lax.fori_loop(half_tiles, n_tiles, unit, 0)
    for i in range(max(n_tiles - 2, 0), n_tiles):
        staged(i % 2, pl.ds(0, mt), pl.ds(0, ft)).wait()
    for gw in (g_o, g_f2):
        gw.arrive()

    h_chain.finish()

    def output(i, _):
        rows_i, cols_i = aligned(lax.div(i, width // wt), mt), aligned(lax.rem(i, width // wt), wt)
        part[rows_i, cols_i] = (
            dot_nn(act[rows_i, :], vf2[:, cols_i]) + dot_nn(att[rows_i, :], vo[:, cols_i])
        ).astype(BF16)
        return 0

    lax.fori_loop(0, (length // mt) * (width // wt), output, 0)
    for st in range(count - 1):
        fold_out.first(True, st, rows_of(part, last - st))
        fold_out.first(False, st, rows_of(part, st))
    fetch_cot.wait()


    def unit_back(j):
        rows_j = aligned(j, rows)
        def body(i, _):
            cols_i = aligned(i, ft)
            low = (dot_nt(g[rows_j, :], vf2[cols_i, :]) * dg[rows_j, cols_i].astype(F32)).astype(BF16)
            dg[rows_j, cols_i] = low
            to = pl.ds(pl.multiple_of(at_f1 + i * ft, LANES), ft)
            vec[:, to] += jnp.sum(low.astype(F32), axis=0, keepdims=True)
            return 0

        lax.fori_loop(0, per_row, body, 0)
        att[rows_j, :] = dot_nt(g[rows_j, :], vo[...]).astype(BF16)
        vec[:, at_ob:at_gain] += jnp.sum(g[rows_j, :].astype(F32), axis=0, keepdims=True)

    c_chain.by_distance(0, 2 * count - 1, unit_back)
    g_o.finish()
    g_f2.finish()
    c_chain.finish()
    load_act = pltpu.make_async_copy(act_t, act_v, act_sem)
    load_act.start()
    hand_over(pair_free)
    own_part = lambda up, d: rows_of(part, d)
    load_act.wait()
    if count > 2:
        fold_out.pump(1, own_part, rows)
    sc_f2.run()
    sc_o.run()
    for k in range(2, count - 1):
        fold_out.pump(k, own_part, rows)


    def key_of(lo, hi):
        seg = segs[lo:hi, 0:1].astype(F32)
        return jnp.where(seg == 0.0, -1.0, seg)

    def turn_back(y, at):
        return y * tab_c[at, :] - swapped(y) * tab_s[at, :]

    def attend_back(pair, _):
        q_cols = aligned(pair, LANES)
        k_cols, v_cols = aligned(pairs + pair, LANES), aligned(2 * pairs + pair, LANES)
        lane = lax.broadcasted_iota(jnp.int32, (1, LANES), 1)
        dk_acc[...] = jnp.zeros_like(dk_acc)
        dv_acc[...] = jnp.zeros_like(dv_acc)
        k_t[...] = qkv[:, k_cols].T
        for b in range(length // qb):
            here, reach = slice(b * qb, (b + 1) * qb), (b + 1) * qb
            before = b * qb
            q2, g2 = qkv[here, q_cols], att[here, q_cols]
            ki = lax.broadcasted_iota(jnp.int32, (qb, qb), 0)
            qi = lax.broadcasted_iota(jnp.int32, (qb, qb), 1)
            seen_here = jnp.logical_or(
                jnp.logical_and(key_of(before, reach) == row_segs[:, here], ki <= qi), ki == qi
            )
            dq_t = []
            for h in range(2):
                mine = (lane // HEAD_DIM) == h
                qh, gh = jnp.where(mine, q2, BF16(0)), jnp.where(mine, g2, BF16(0))
                stat = lse[pl.ds(2 * pair + h, 1), here]
                spans = ([(0, before)] if before else []) + [(before, reach)]
                probs, grads = [], []
                delta = jnp.zeros((1, qb), F32)
                for lo, hi in spans:
                    seen = seen_here if lo == before else key_of(lo, hi) == row_segs[:, here]
                    p = jnp.exp(jnp.where(seen, dot_nt(qkv[lo:hi, k_cols], qh), NEGATIVE) - stat)
                    pg = dot_nt(qkv[lo:hi, v_cols], gh)
                    delta = delta + jnp.sum(p * pg, axis=0, keepdims=True)
                    probs.append(p)
                    grads.append(pg)
                acc = jnp.zeros((HEAD_DIM, qb), F32)
                for (lo, hi), p, pg in zip(spans, probs, grads):
                    sg = (p * (pg - delta)).astype(BF16)
                    dv_acc[lo:hi, :] += dot_nn(p.astype(BF16), gh)
                    dk_acc[lo:hi, :] += dot_nn(sg, qh)
                    acc = acc + dot_nn(k_t[h * HEAD_DIM : (h + 1) * HEAD_DIM, lo:hi], sg)
                dq_t.append(acc)
            dq = jnp.concatenate(dq_t, axis=0).T * HEAD_DIM**-0.5
            qkv[here, q_cols] = turn_back(dq, here).astype(BF16)
        for b in range(length // qb):
            here = slice(b * qb, (b + 1) * qb)
            qkv[here, k_cols] = turn_back(dk_acc[here, :], here).astype(BF16)
            qkv[here, v_cols] = dv_acc[here, :].astype(BF16)
        for cols in (q_cols, k_cols, v_cols):
            vec[:, cols] = jnp.sum(qkv[:, cols].astype(F32), axis=0, keepdims=True)
        return 0

    lax.fori_loop(0, pairs, attend_back, 0)

    def hidden_back(d):
        here = pl.ds(d * rows, rows)

        def body(i, _):
            cols_i = aligned(i, wt)
            g[here, cols_i] = (
                dot_nt(dg[here, :], vf1[cols_i, :]) + dot_nt(qkv[here, :], vqkv[cols_i, :])
            ).astype(BF16)
            return 0

        lax.fori_loop(0, width // wt, body, 0)

    def set_out(d):
        if d > 0:
            fold_hid.first(True, last - d, rows_of(g, d))
        if d < last:
            fold_hid.first(False, d, rows_of(g, d))

    dests = list(dict.fromkeys(d for both in zip(range(last, -1, -1), range(count)) for d in both))
    fold_out.arrive()
    def finish_output(i, _):
        part = aligned(i, 32)
        at = pl.ds(pl.multiple_of(z * rows + i * 32, 32), 32)
        y = fold_out.total(hid[at, :].astype(F32), part)
        hid[at, :] = (x[part, :].astype(F32) + y + out_bias[...]).astype(BF16)
        return 0

    lax.fori_loop(0, rows // 32, finish_output, 0)
    save_out = pltpu.make_async_copy(hid.at[aligned(z, rows), :], block_out, out_sem)
    save_out.start()
    fold_out.finish()

    @pl.when(z > 0)
    def _():
        pl.semaphore_signal(free_up, inc=1, device_id=(dp, z - 1), device_id_type=MESH)

    @pl.when(z < last)
    def _():
        pl.semaphore_signal(free_dn, inc=1, device_id=(dp, z + 1), device_id_type=MESH)

    @pl.when(z < last)
    def _():
        pl.semaphore_wait(free_up, 1)

    @pl.when(z > 0)
    def _():
        pl.semaphore_wait(free_dn, 1)

    for d in dests:
        hidden_back(d)
        set_out(d)
    own_grad = lambda up, d: rows_of(g, d)
    run_rows(sc_f1, (lambda: fold_hid.pump(1, own_grad, rows)) if count > 2 else None)
    save_out.wait()
    hand_over(hid_free)
    run_rows(sc_qkv)
    sc_f2.sent()
    load_cot = pltpu.make_async_copy(cot, vf2.at[0:rows, 0:width], cot_sem)
    load_cot.start()
    for k in range(2, count - 1):
        fold_hid.pump(k, own_grad, rows)
    fold_hid.arrive()
    load_cot.wait()

    step_rows = 16

    def ig_copy(i, slot):
        return pltpu.make_async_copy(ig_stage.at[slot], input_grad.at[aligned(i, step_rows), :], ig_sem.at[slot])

    def norm_back(i, _):
        part = aligned(i, step_rows)
        slot = lax.rem(i, 2)
        inputs = x[part, :].astype(F32)
        center = inputs - jnp.mean(inputs, axis=-1, keepdims=True)
        inverse = lax.rsqrt(jnp.mean(center * center, axis=-1, keepdims=True) + EPSILON)
        normed = center * inverse
        own = g[pl.ds(pl.multiple_of(z * rows + i * step_rows, step_rows), step_rows), :].astype(F32)
        y = fold_hid.total(own, part)
        vec[:, at_gain : at_gain + width] += jnp.sum(y * normed, axis=0, keepdims=True)
        vec[:, at_beta : at_beta + width] += jnp.sum(y, axis=0, keepdims=True)
        scaled = y * gain[...]
        result = vf2[part, :].astype(F32) + inverse * (
            scaled
            - jnp.mean(scaled, axis=-1, keepdims=True)
            - normed * jnp.mean(scaled * normed, axis=-1, keepdims=True)
        )

        @pl.when(i >= 2)
        def _():
            ig_copy(i, slot).wait()

        ig_stage[slot] = result
        ig_copy(i, slot).start()
        return 0

    steps = rows // step_rows
    lax.fori_loop(0, steps, norm_back, 0)

    to_pair = pltpu.make_async_remote_copy(
        src_ref=vec, dst_ref=vec_pair, send_sem=v_ps, recv_sem=v_pr,
        device_id=(chip * 2 + 1 - core, z), device_id_type=MESH,
    )
    to_pair.start()
    for i in range(max(steps - 2, 0), steps):
        ig_copy(i, i % 2).wait()
    to_pair.wait()
    vec_chip[chip] = vec[...] + vec_pair[...]

    def chip_copy(r, slot):
        return pltpu.make_async_remote_copy(
            src_ref=vec_chip.at[chip], dst_ref=vec_chip.at[slot], send_sem=v_cs.at[r - 1], recv_sem=v_cr.at[r - 1],
            device_id=(flip(chip, r) * 2 + core, z), device_id_type=MESH,
        )

    for r in range(1, chips):
        chip_copy(r, chip).start()
    for r in range(1, chips):
        chip_copy(r, flip(chip, r)).wait_recv()
    total = vec_chip[0]
    for c in range(1, chips):
        total = total + vec_chip[c]
    vec_out[:, 0:at_gain] = total[:, 0:at_gain]
    vec_z[z] = total[:, at_gain:]

    def z_copy(shift, slot):
        return pltpu.make_async_remote_copy(
            src_ref=vec_z.at[z], dst_ref=vec_z.at[slot], send_sem=v_zs.at[shift - 1], recv_sem=v_zr.at[shift - 1],
            device_id=(dp, lax.rem(z + shift, count)), device_id_type=MESH,
        )

    for shift in range(1, count):
        z_copy(shift, z).start()
    for shift in range(1, count):
        z_copy(shift, lax.rem(z + count - shift, count)).wait_recv()
    total = vec_z[0]
    for n in range(1, count):
        total = total + vec_z[n]
    vec_out[:, at_gain:] = total
    for r in range(1, chips):
        chip_copy(r, chip).wait_send()
    for shift in range(1, count):
        z_copy(shift, z).wait_send()
    fold_hid.finish()
    for s in (sc_f1, sc_o, sc_qkv):
        s.sent()
    for s in (sc_f2, sc_f1, sc_o, sc_qkv):
        s.finish()
    for gw in (*g_qkv, g_f1):
        gw.finish()


def run_block(ndp, count, x, gain, beta, bqkv, bf1, out_bias, seg_row, frequency, wq, wk, wv, wf1, wo, wf2, cot):
    chips = ndp // 2
    rows, width = x.shape
    length = rows * count
    hcols, units = wo.shape[0], wf2.shape[0]
    part_w = width // ndp
    total = 3 * hcols + units + 3 * width
    heads = hcols // HEAD_DIM
    mt, ft, wt = tile_of(length), tile_of(units), tile_of(width)
    anywhere = pl.BlockSpec(memory_space=pl.ANY)
    vmem = pl.BlockSpec(memory_space=pltpu.VMEM)
    low = lambda *shape: jax.ShapeDtypeStruct(shape, BF16)
    wide = lambda *shape: jax.ShapeDtypeStruct(shape, F32)
    outs = [
        low(rows, width), wide(rows, width), wide(1, total),
        wide(part_w, 3 * hcols), wide(part_w, units), wide(hcols, part_w), wide(units, part_w),
        low(chips - 1, part_w, 3 * hcols), low(chips - 1, part_w, units), low(chips - 1, hcols, part_w), low(chips - 1, units, part_w),
        low(width, length), low(units, length),
    ]
    v = lambda *shape: pltpu.VMEM(shape, BF16)
    w = lambda *shape: pltpu.VMEM(shape, F32)
    steps = max(count - 1, 1)
    dma = lambda *shape: pltpu.SemaphoreType.DMA(shape)
    one, plain = pltpu.SemaphoreType.DMA, pltpu.SemaphoreType.REGULAR
    row_tile = max(piece_of(units), piece_of(3 * hcols))
    col_tile = max(piece_of(units), piece_of(hcols))
    scratch = [
        v(length, width), v(width, 3 * hcols), v(width, units), v(units, width), v(hcols, width),
        v(length, 3 * hcols), v(length, hcols), v(hcols, length), w(heads, length), v(length, units), v(length, units),
        v(length, width), v(2, max(ft, wt, part_w), max(mt, part_w)), w(length, LANES), w(length, LANES), v(length, LANES),
        w(length, LANES), w(length, LANES), v(LANES, length), v(steps, rows, width), v(steps, rows, width),
        w(part_w, row_tile), w(col_tile, part_w),
        w(2, 16, width), w(1, total), w(1, total), w(chips, 1, total), w(count, 1, 2 * width),
        dma(6, chips - 1), dma(6, chips - 1), dma(6, 2), dma(6, 2), dma(6, chips), dma(6, chips), dma(6),
        *[dma(steps) for _ in range(8)], one, dma(2),
        one, dma(2), one, dma(2), dma(2), dma(2),
        dma(4, chips), dma(4, chips - 1), dma(4, chips - 1), one, one,
        *[dma(steps) for _ in range(8)], plain, plain, plain, plain,
        one, one, dma(chips - 1), dma(chips - 1), dma(steps), dma(steps),
    ]
    return pl.pallas_call(
        functools.partial(block_kernel, chips, count),
        out_shape=outs,
        in_specs=[vmem] * 8 + [anywhere] * 7,
        out_specs=[anywhere, anywhere, vmem] + [anywhere] * 10,
        scratch_shapes=scratch,
        compiler_params=pltpu.CompilerParams(
            collective_id=0, has_side_effects=True, vmem_limit_bytes=VMEM_LIMIT
        ),
        name="block_step",
    )(x, gain, beta, bqkv, bf1, out_bias, seg_row, frequency, wq, wk, wv, wf1, wo, wf2, cot)[:11]


def on_device(
    ndp, count,
    block_input, segment_ids, out_cotangent, norm_gain, norm_bias, query_weight, key_weight, value_weight,
    query_bias, key_bias, value_bias, out_weight, fc1_weight, fc1_bias, fc2_weight, output_bias,
):
    x = block_input[0]
    cot = out_cotangent[0]
    width = x.shape[1]
    half_rot = ROT // 2
    frequency = 10000.0 ** (-2.0 * (jnp.arange(LANES, dtype=jnp.int32) % half_rot).astype(F32) / ROT)
    bqkv = jnp.concatenate([query_bias, key_bias, value_bias])[None, :]
    gain, seg_row = norm_gain[None, :], segment_ids
    (block_output, input_grad, vec, own_qkv, own_f1, own_o, own_f2, land_qkv, land_f1, land_o, land_f2) = run_block(
        ndp, count, x, gain, norm_bias[None, :], bqkv, fc1_bias[None, :], output_bias[None, :], seg_row,
        frequency[None, :], query_weight, key_weight, value_weight, fc1_weight, out_weight, fc2_weight, cot,
    )
    hcols, units = out_weight.shape[0], fc2_weight.shape[0]

    def summed(own, landed):
        for n in range(landed.shape[0]):
            own = own + landed[n].astype(F32)
        return own

    def third(i):
        cols = slice(i * hcols, (i + 1) * hcols)
        return summed(own_qkv[:, cols], land_qkv[:, :, cols])

    sizes = (hcols, hcols, hcols, units, width, width, width)
    pieces, at = [], 0
    for size in sizes:
        pieces.append(vec[0, at : at + size])
        at += size
    qb, kb, vb, f1b, ob, gain_grad, beta_grad = pieces
    return (
        block_output[None], input_grad[None], gain_grad, beta_grad,
        third(0), third(1), third(2), qb, kb, vb,
        summed(own_o, land_o), summed(own_f1, land_f1), f1b, summed(own_f2, land_f2), ob,
    )


def solution(mesh):
    tokens, vector, split = P("dp", "branch", None), P(), P("branch")
    rows_first, cols_first = P("dp", "branch"), P("branch", "dp")
    in_specs = (
        tokens, P("dp", None), tokens, vector, vector, rows_first, rows_first, rows_first,
        split, split, split, cols_first, rows_first, split, cols_first, vector,
    )
    out_specs = (
        tokens, tokens, vector, vector, rows_first, rows_first, rows_first, split, split, split,
        cols_first, rows_first, split, cols_first, vector,
    )
    return jax.shard_map(
        functools.partial(on_device, mesh.shape["dp"], mesh.shape["branch"]),
        mesh=mesh, in_specs=in_specs, out_specs=out_specs, check_vma=False,
    )
```

time: 391 us -> 371 us (0.949)
  Pallas kernels: 363 us -> 344 us
    pallas_call x2 -> x1, Pallas kernels: 363 us -> 344 us  [run_block(): pl.pallas_call(functools.partial(block_kernel, chips, count), out_shape=o...]
where the time goes in v1:
time: 371 us; the launch traced here: 364 us
  Pallas kernels  344 us (93%)
  other arithmetic  10.2 us (3%)
  local copies, waits for them, and re-layouts  8.73 us (2%)
    pallas_call x1, Pallas kernels, run_block(): pl.pallas_call(functools.partial(block_kernel, chips, count), out_shape=o...  344 us
    add x4, other arithmetic, summed(): own = own + landed[n].astype(F32)  8.94 us

profile of v1, /device:TPU:0, one launch (start us, length us, event | category | flops | bytes accessed | tf_op | source)
XLA Modules:
  0.0 363.9 jit_solution(462506853712008531)
XLA Ops:
  0.6 0.5 fusion.2.frequency
  1.2 0.7 pad_maximum_fusion
  1.9 0.6 broadcast_in_dim.24.bqkv
  2.5 343.8 %block_step.1 = (bf16[256,2048]{1,0:T(8,128)(2,1)}, f32[256,2048]{1,0:T(8,128)}, f32[1,9728]{1,0:T(1,128)}, f32[256,1536]{1,0:T(8,128)}, f32[256,2048]{1,0:T(8,1...) custom-call(bf16[256,2048]{1,0:T(8,128)(2,1)} %bitcast.70, ...), custom_call_target="tpu_custom_call" | custom-call | tf_op jit(solution)/shard_map/block_step/pallas_call | solution.py:1039
  346.3 0.0 copy-start.5
  346.3 1.4 fusion.4
  347.7 1.4 fusion.3
  349.1 2.2 convert_add_fusion.6
  351.3 0.0 copy-done.5
  351.3 0.0 copy-start.1
  351.3 0.0 copy-start.3
  351.3 3.1 convert_add_fusion.9
  354.4 0.0 copy-done.1
  354.4 0.7 copy-done.3
  355.1 0.0 copy-start
  355.1 0.0 copy-start.2
  355.1 1.9 convert_add_fusion.3
  357.0 0.7 copy-done
  357.7 0.7 copy-done.2
  358.4 0.0 copy-start.6
  358.4 1.7 convert_add_fusion
  360.1 0.0 copy-done.6
  360.1 0.0 copy-start.4
  360.1 1.0 copy.33
  361.1 1.0 copy-done.4
  362.1 1.3 copy.34
Async XLA Ops:
  346.3 4.9 %copy-start.5 = (f32[256,1536]{1,0:T(8,128)S(1)}, f32[256,1536]{1,0:T(8,128)}, u32[]{:S(2)}) copy-start(f32[256,1536]{1,0:T(8,128)} %get-tuple-element.29) | copy-start | bytes 4718596
  351.3 3.1 copy-start.1
  351.3 3.8 %copy-start.3 = (f32[256,2048]{1,0:T(8,128)S(1)}, f32[256,2048]{1,0:T(8,128)}, u32[]{:S(2)}) copy-start(f32[256,2048]{1,0:T(8,128)} %get-tuple-element.33) | copy-start | bytes 6291460
  355.1 2.6 copy-start
  355.1 3.3 copy-start.2
  358.4 1.7 copy-start.6
  360.1 2.0 copy-start.4

commit v2 on v1

--- a/solution.py
+++ b/solution.py
@@ -247,14 +247,15 @@
     def dest(self, up, step):
         return self.count - 1 - step if up else step
 
-    def hop(self, up, step, src=None):
+    def hop(self, up, step, half, src=None):
         buf = self.bufs[0 if up else 1]
         send, recv = self.sems[0 if up else 2], self.sems[1 if up else 3]
+        rows = pl.ds(half * (buf.shape[1] // 2), buf.shape[1] // 2)
         return pltpu.make_async_remote_copy(
-            src_ref=buf.at[step] if src is None else src,
-            dst_ref=buf.at[step],
-            send_sem=send.at[step],
-            recv_sem=recv.at[step],
+            src_ref=buf.at[step, rows, :] if src is None else src.at[rows, :],
+            dst_ref=buf.at[step, rows, :],
+            send_sem=send.at[step, half],
+            recv_sem=recv.at[step, half],
             device_id=(self.dp, self.z + 1 if up else self.z - 1),
             device_id_type=MESH,
         )
@@ -262,7 +263,8 @@
     def first(self, up, step, src):
         @pl.when(self.place(up) == 0)
         def _():
-            self.hop(up, step, src).start()
+            for half in range(2):
+                self.hop(up, step, half, src).start()
 
     def pump(self, k, own_block, rows):
         for up in (False, True):
@@ -272,16 +274,17 @@
             def _(up=up, place=place):
                 step = k - place
                 own = own_block(up, self.dest(up, step))
-                self.hop(up, step).wait_recv()
                 buf = self.bufs[0 if up else 1]
-
-                def add(i, _):
-                    part = aligned(i, 32)
-                    buf[step, part, :] = (buf[step, part, :].astype(F32) + own[part, :].astype(F32)).astype(BF16)
-                    return 0
-
-                lax.fori_loop(0, rows // 32, add, 0)
-                self.hop(up, step).start()
+                for half in range(2):
+                    self.hop(up, step, half).wait_recv()
+
+                    def add(i, _):
+                        part = aligned(i, 32)
+                        buf[step, part, :] = (buf[step, part, :].astype(F32) + own[part, :].astype(F32)).astype(BF16)
+                        return 0
+
+                    lax.fori_loop(half * (rows // 64), (half + 1) * (rows // 64), add, 0)
+                    self.hop(up, step, half).start()
 
     def last_step(self, up):
         return jnp.clip(self.count - 1 - self.place(up), 0, self.count - 2)
@@ -291,7 +294,8 @@
 
             @pl.when(self.place(up) >= 1)
             def _(up=up):
-                self.hop(up, self.last_step(up)).wait_recv()
+                for half in range(2):
+                    self.hop(up, self.last_step(up), half).wait_recv()
 
     def total(self, own, part):
         out = own
@@ -306,23 +310,26 @@
 
                 @pl.when(self.place(up) + step <= self.count - 2)
                 def _(up=up, step=step):
-                    self.hop(up, step).wait_send()
+                    for half in range(2):
+                        self.hop(up, step, half).wait_send()
 
 
 class Scatter:
-    def __init__(self, index, block, tile, rows_first, base, size, landing, own_out, stage, wide, chips, sems):
+    def __init__(self, index, block, tile, rows_first, base, size, relays, landing, own_out, stage, wide, chips, sems):
         self.index, self.block, self.tile, self.rows_first = index, block, tile, rows_first
         self.base, self.size, self.landing, self.own_out = base, size, landing, own_out
         self.stage, self.wide = stage, wide
         self.chips = chips
-        self.st_sem, self.pair_recv, self.send, self.recv, self.wide_sem = sems
+        self.relays = relays
+        self.st_sem, self.pair_recv, self.send, self.recv, self.wide_sem, self.r_send, self.r_recv, self.r_load = sems
         dp = lax.axis_index("dp")
         self.z = lax.axis_index("branch")
         self.core, self.chip = lax.rem(dp, 2), lax.div(dp, 2)
         self.tiles = size[1 if rows_first else 0] // tile
         self.height = size[0] if rows_first else tile
         self.breadth = tile if rows_first else size[1]
-        self.order = [*range(1, chips), 0]
+        self.relayed = chips == 4
+        self.order = [3, 1, 2, 0] if self.relayed else [*range(1, chips), 0]
 
     def slot(self, r):
         high, wide = self.size
@@ -362,15 +369,74 @@
             device_id_type=MESH,
         )
 
-    def to_owner(self, r):
+    def half(self, r, which):
+        high, wide = self.size
+        if self.rows_first:
+            return self.base.at[pl.ds(r * high + which * (high // 2), high // 2), 0:wide]
+        return self.base.at[pl.ds(which * (high // 2), high // 2), r * wide : (r + 1) * wide]
+
+    def to_owner(self, r, which=None):
+        high = self.size[0]
+        at = (r - 1) if which is None else 2 * (r - 1) + which
+        rows = pl.ds(0, high) if which is None else pl.ds(which * (high // 2), high // 2)
         return pltpu.make_async_remote_copy(
-            src_ref=self.slot(r),
-            dst_ref=self.landing.at[r - 1],
-            send_sem=self.send.at[self.index, r - 1],
-            recv_sem=self.recv.at[self.index, r - 1],
+            src_ref=self.slot(r) if which is None else self.half(r, which),
+            dst_ref=self.landing.at[r - 1, rows, :],
+            send_sem=self.send.at[self.index, at],
+            recv_sem=self.recv.at[self.index, at],
             device_id=(flip(self.chip, r) * 2 + self.core, self.z),
             device_id_type=MESH,
         )
+
+    def to_relay(self, which):
+        return pltpu.make_async_remote_copy(
+            src_ref=self.half(3, which),
+            dst_ref=self.relays.at[which],
+            send_sem=self.r_send.at[self.index, which],
+            recv_sem=self.r_recv.at[self.index, which],
+            device_id=(flip(self.chip, 1 + which) * 2 + self.core, self.z),
+            device_id_type=MESH,
+        )
+
+    def relay(self):
+        if not self.relayed:
+            return
+        high, wide = self.size
+        tall = high // 2 if self.rows_first else min(self.tile, high // 2)
+        broad = self.tile if self.rows_first else wide
+        pieces = wide // broad if self.rows_first else (high // 2) // tall
+        for which in range(2):
+            r = 2 - which
+            self.to_relay(which).wait_recv()
+
+            def fetch(i):
+                rows = pl.ds(0, tall) if self.rows_first else aligned(i, tall)
+                cols = aligned(i, broad) if self.rows_first else pl.ds(0, wide)
+                slot = lax.rem(i, 2)
+                return pltpu.make_async_copy(
+                    self.relays.at[which, rows, cols],
+                    self.stage.at[slot, pl.ds(0, tall), pl.ds(0, broad)],
+                    self.r_load.at[slot],
+                )
+
+            def body(i, _):
+                @pl.when(i + 1 < pieces)
+                def _():
+                    fetch(i + 1).start()
+
+                fetch(i).wait()
+                if self.rows_first:
+                    at = (pl.ds(r * high + which * tall, tall), aligned(i, broad))
+                else:
+                    top = which * (high // 2)
+                    at = (pl.ds(pl.multiple_of(top + i * tall, tall), tall), pl.ds(r * wide, wide))
+                got = self.stage[lax.rem(i, 2), 0:tall, 0:broad].astype(F32)
+                self.base[at] = (self.base[at].astype(F32) + got).astype(BF16)
+                return 0
+
+            fetch(0).start()
+            lax.fori_loop(0, pieces, body, 0)
+            self.to_owner(r, which).start()
 
     def to_out(self, i):
         source = self.wide.at[0 : self.height, 0 : self.breadth]
@@ -418,8 +484,13 @@
             return 0
 
         lax.fori_loop(0, self.tiles, body, 0)
-        if r:
+        if r and not self.relayed:
             self.to_owner(r).start()
+        elif r == 3:
+            self.to_relay(0).start()
+            self.to_relay(1).start()
+        elif r:
+            self.to_owner(r, r - 1).start()
         else:
             self.to_out(self.tiles - 1).wait()
 
@@ -437,13 +508,18 @@
         for i in range(max(total - 2, 0), total):
             self.to_pair(0, 0, i % 2).wait_send()
 
+    def all(self):
+        if self.relayed:
+            return [self.to_owner(r, which) for r in (1, 2) for which in range(2)]
+        return [self.to_owner(r) for r in range(1, self.chips)]
+
     def sent(self):
-        for r in range(1, self.chips):
-            self.to_owner(r).wait_send()
+        for c in self.all() + ([self.to_relay(0), self.to_relay(1)] if self.relayed else []):
+            c.wait_send()
 
     def finish(self):
-        for r in range(1, self.chips):
-            self.to_owner(r).wait_recv()
+        for c in self.all():
+            c.wait_recv()
 
 
 def piece_of(extent):
@@ -453,12 +529,12 @@
 def block_kernel(
     chips, count,
     x, gain, beta, bqkv, bf1, out_bias, seg_row, frequency, wq, wk, wv, wf1, wo, wf2, cot,
-    block_out, input_grad, vec_out, own_qkv, own_f1, own_o, own_f2, land_qkv, land_f1, land_o, land_f2, hid_t, act_t,
+    block_out, input_grad, vec_out, own_qkv, own_f1, own_o, own_f2, land_qkv, land_f1, land_o, land_f2, hid_t, act_t, rel_qkv, rel_f1, rel_o, rel_f2,
     hid, vqkv, vf1, vf2, vo, qkv, att, att_t, lse, act, dg, g, stage, tab_c, tab_s, segs,
     dk_acc, dv_acc, k_t, up_buf, dn_buf, wide_row, wide_col, ig_stage, vec, vec_pair, vec_chip, vec_z,
     w_send, w_recv, r_send, r_recv, p_send, p_recv, own_sem,
     h_us, h_ur, h_ds, h_dr, c_us, c_ur, c_ds, c_dr, cot_sem, st_sem,
-    act_sem, hid_sem, out_sem, ig_sem, st_row_sem, st_col_sem, pair_recv, x_send, x_recv, wide_row_sem, wide_col_sem,
+    act_sem, hid_sem, out_sem, ig_sem, st_row_sem, st_col_sem, pair_recv, x_send, x_recv, wide_row_sem, wide_col_sem, rl_send, rl_recv, rl_load,
     zo_us, zo_ur, zo_ds, zo_dr, zh_us, zh_ur, zh_ds, zh_dr, free_up, free_dn, pair_free, hid_free,
     v_ps, v_pr, v_cs, v_cr, v_zs, v_zr,
 ):
@@ -496,8 +572,8 @@
         pl.semaphore_signal(free, inc=1, device_id=(chip * 2 + 1 - core, z), device_id_type=MESH)
         pl.semaphore_wait(free, 1)
 
-    sems_row = (st_row_sem, pair_recv, x_send, x_recv, wide_row_sem)
-    sems_col = (st_col_sem, pair_recv, x_send, x_recv, wide_col_sem)
+    sems_row = (st_row_sem, pair_recv, x_send, x_recv, wide_row_sem, rl_send, rl_recv, rl_load)
+    sems_col = (st_col_sem, pair_recv, x_send, x_recv, wide_col_sem, rl_send, rl_recv, rl_load)
     tile_f2, tile_o = piece_of(units), piece_of(hcols)
     tile_f1, tile_qkv = piece_of(units), piece_of(3 * hcols)
 
@@ -538,10 +614,10 @@
                 between()
         scatter.drain()
 
-    sc_f2 = Scatter(0, f2_block, tile_f2, False, vf2, (units, part_w), land_f2, own_f2, stage, wide_col, chips, sems_col)
-    sc_f1 = Scatter(1, f1_block, tile_f1, True, act, (part_w, units), land_f1, own_f1, stage, wide_row, chips, sems_row)
-    sc_o = Scatter(2, o_block, tile_o, False, vo, (hcols, part_w), land_o, own_o, stage, wide_col, chips, sems_col)
-    sc_qkv = Scatter(3, qkv_block, tile_qkv, True, hid, (part_w, 3 * hcols), land_qkv, own_qkv, stage, wide_row, chips, sems_row)
+    sc_f2 = Scatter(0, f2_block, tile_f2, False, vf2, (units, part_w), rel_f2, land_f2, own_f2, stage, wide_col, chips, sems_col)
+    sc_f1 = Scatter(1, f1_block, tile_f1, True, act, (part_w, units), rel_f1, land_f1, own_f1, stage, wide_row, chips, sems_row)
+    sc_o = Scatter(2, o_block, tile_o, False, vo, (hcols, part_w), rel_o, land_o, own_o, stage, wide_col, chips, sems_col)
+    sc_qkv = Scatter(3, qkv_block, tile_qkv, True, hid, (part_w, 3 * hcols), rel_qkv, land_qkv, own_qkv, stage, wide_row, chips, sems_row)
 
     greet(chips, count)
     for gw in (*g_qkv, g_f1):
@@ -864,6 +940,9 @@
             fold_hid.first(False, d, rows_of(g, d))
 
     dests = list(dict.fromkeys(d for both in zip(range(last, -1, -1), range(count)) for d in both))
+    for d in dests[:2]:
+        hidden_back(d)
+
     fold_out.arrive()
     def finish_output(i, _):
         part = aligned(i, 32)
@@ -893,19 +972,29 @@
     def _():
         pl.semaphore_wait(free_dn, 1)
 
-    for d in dests:
+    for d in dests[:2]:
+        set_out(d)
+    sc_f2.relay()
+    sc_o.relay()
+    for d in dests[2:]:
         hidden_back(d)
         set_out(d)
     own_grad = lambda up, d: rows_of(g, d)
-    run_rows(sc_f1, (lambda: fold_hid.pump(1, own_grad, rows)) if count > 2 else None)
+
+    def pump_hidden(lo, hi):
+        for k in range(lo, hi):
+            fold_hid.pump(k, own_grad, rows)
+
+    pump_hidden(1, min(2, count - 1))
+    run_rows(sc_f1)
     save_out.wait()
     hand_over(hid_free)
-    run_rows(sc_qkv)
+    run_rows(sc_qkv, lambda: pump_hidden(2, count - 1))
+    sc_f1.relay()
     sc_f2.sent()
     load_cot = pltpu.make_async_copy(cot, vf2.at[0:rows, 0:width], cot_sem)
     load_cot.start()
-    for k in range(2, count - 1):
-        fold_hid.pump(k, own_grad, rows)
+    sc_qkv.relay()
     fold_hid.arrive()
     load_cot.wait()
 
@@ -1003,6 +1092,7 @@
     hcols, units = wo.shape[0], wf2.shape[0]
     part_w = width // ndp
     total = 3 * hcols + units + 3 * width
+    lands = 2 if chips == 4 else chips - 1
     heads = hcols // HEAD_DIM
     mt, ft, wt = tile_of(length), tile_of(units), tile_of(width)
     anywhere = pl.BlockSpec(memory_space=pl.ANY)
@@ -1012,8 +1102,9 @@
     outs = [
         low(rows, width), wide(rows, width), wide(1, total),
         wide(part_w, 3 * hcols), wide(part_w, units), wide(hcols, part_w), wide(units, part_w),
-        low(chips - 1, part_w, 3 * hcols), low(chips - 1, part_w, units), low(chips - 1, hcols, part_w), low(chips - 1, units, part_w),
+        low(lands, part_w, 3 * hcols), low(lands, part_w, units), low(lands, hcols, part_w), low(lands, units, part_w),
         low(width, length), low(units, length),
+        low(2, part_w // 2, 3 * hcols), low(2, part_w // 2, units), low(2, hcols // 2, part_w), low(2, units // 2, part_w),
     ]
     v = lambda *shape: pltpu.VMEM(shape, BF16)
     w = lambda *shape: pltpu.VMEM(shape, F32)
@@ -1032,15 +1123,15 @@
         dma(6, chips - 1), dma(6, chips - 1), dma(6, 2), dma(6, 2), dma(6, chips), dma(6, chips), dma(6),
         *[dma(steps) for _ in range(8)], one, dma(2),
         one, dma(2), one, dma(2), dma(2), dma(2),
-        dma(4, chips), dma(4, chips - 1), dma(4, chips - 1), one, one,
-        *[dma(steps) for _ in range(8)], plain, plain, plain, plain,
+        dma(4, chips), dma(4, max(chips - 1, 4)), dma(4, max(chips - 1, 4)), one, one, dma(4, 2), dma(4, 2), dma(2),
+        *[dma(steps, 2) for _ in range(8)], plain, plain, plain, plain,
         one, one, dma(chips - 1), dma(chips - 1), dma(steps), dma(steps),
     ]
     return pl.pallas_call(
         functools.partial(block_kernel, chips, count),
         out_shape=outs,
         in_specs=[vmem] * 8 + [anywhere] * 7,
-        out_specs=[anywhere, anywhere, vmem] + [anywhere] * 10,
+        out_specs=[anywhere, anywhere, vmem] + [anywhere] * 14,
         scratch_shapes=scratch,
         compiler_params=pltpu.CompilerParams(
             collective_id=0, has_side_effects=True, vmem_limit_bytes=VMEM_LIMIT

time: 371 us -> 375 us (1.011); the launches traced: 364 us -> 373 us
  Pallas kernels: 344 us -> 355 us
    pallas_call x1, Pallas kernels: 344 us -> 355 us  [run_block(): pl.pallas_call(functools.partial(block_kernel, chips, count), out_shape=o...]
where the time goes in v2:
time: 375 us; the launch traced here: 373 us
  Pallas kernels  355 us (95%)
  other arithmetic  9.48 us (3%)
  local copies, waits for them, and re-layouts  8.01 us (2%)
    pallas_call x1, Pallas kernels, run_block(): pl.pallas_call(functools.partial(block_kernel, chips, count), out_shape=o...  355 us
    add x4, other arithmetic, summed(): own = own + landed[n].astype(F32)  8.24 us

profile of v2, /device:TPU:0, one launch (start us, length us, event | category | flops | bytes accessed | tf_op | source)
XLA Modules:
  0.0 373.2 jit_solution(6428761823869056300)
XLA Ops:
  0.6 0.5 fusion.2.frequency
  1.2 0.7 pad_maximum_fusion
  1.9 0.6 broadcast_in_dim.24.bqkv
  2.5 354.8 %block_step.1 = (bf16[256,2048]{1,0:T(8,128)(2,1)}, f32[256,2048]{1,0:T(8,128)}, f32[1,9728]{1,0:T(1,128)}, f32[256,1536]{1,0:T(8,128)}, f32[256,2048]{1,0:T(8,1...) custom-call(bf16[256,2048]{1,0:T(8,128)(2,1)} %bitcast.52, ...), custom_call_target="tpu_custom_call" | custom-call | tf_op jit(solution)/shard_map/block_step/pallas_call | solution.py:1130
  357.3 0.0 copy-start.5
  357.3 1.4 fusion.4
  358.7 1.4 fusion.3
  360.1 2.0 convert_add_fusion.4
  362.1 0.0 copy-done.5
  362.1 0.0 copy-start.2
  362.1 0.0 copy-start.3
  362.1 2.8 convert_add_fusion.6
  365.0 0.0 copy-done.2
  365.0 0.1 copy-done.3
  365.1 0.0 copy-start
  365.1 0.0 copy-start.1
  365.1 1.8 convert_add_fusion.2
  366.9 0.2 copy-done
  367.1 1.0 copy-done.1
  368.1 0.0 copy-start.6
  368.1 1.6 convert_add_fusion
  369.7 0.0 copy-done.6
  369.7 0.0 copy-start.4
  369.7 1.0 copy.33
  370.7 1.0 copy-done.4
  371.7 1.3 copy.34
Async XLA Ops:
  357.3 4.8 %copy-start.5 = (f32[256,1536]{1,0:T(8,128)S(1)}, f32[256,1536]{1,0:T(8,128)}, u32[]{:S(2)}) copy-start(f32[256,1536]{1,0:T(8,128)} %get-tuple-element.29) | copy-start | bytes 4718596
  362.1 2.8 copy-start.2
  362.1 3.0 copy-start.3
  365.1 2.0 copy-start
  365.1 3.0 copy-start.1
  368.1 1.6 copy-start.6
  369.7 2.0 copy-start.4
